TPU v7x, 32 devices: a whole 2x2x4 slice. The times are simulated.
32 devices in a mesh: grp: 2 (over x), row: 16 (over z, y, core).
Axes of the slice: x: 2, y: 2, z: 4, core: 2. Of those that a mesh axis runs over, the one named last changes fastest.
Arguments:
- features: bfloat16 [65536, 128], P(('grp', 'row')), parts along dimension 0, may hold values from -6 to 6
- weight: bfloat16 [128, 256], replicated, may hold values from -0.5 to 0.5
- grad_out: bfloat16 [65536, 256], P(('grp', 'row')), parts along dimension 0, may hold values from -6 to 6
- local_vals: bfloat16 [512, 8, 128, 128], P(('grp', 'row')), parts along dimension 0, may hold values from 0 to 1, as said below
- local_cols: int32 [512, 8], P(('grp', 'row')), parts along dimension 0, may hold values from 0 to 15, all different within a row
- remote_vals: bfloat16 [512, 4, 128, 128], P(('grp', 'row')), parts along dimension 0, may hold values from 0 to 1, as said below
- remote_owner: int32 [512, 4], P(('grp', 'row')), parts along dimension 0, may hold values from 0 to 15, all different within a row; in each aligned block of 16 rows (0 to 15, 16 to 31, ...) at most 8 rows name the same one
- remote_index: int32 [512, 4], P(('grp', 'row')), parts along dimension 0, may hold values from 0 to 15
- remote_flag: int32 [512, 4], P(('grp', 'row')), parts along dimension 0, may hold values 0 or 1
Outputs:
- hidden: bfloat16 [65536, 256], P(('grp', 'row')), parts along dimension 0
- input_grad: bfloat16 [65536, 128], P(('grp', 'row')), parts along dimension 0
- weight_grad: float32 [256, 256], P('grp'), parts along dimension 0
There are 2 independent parts, one for each index of `grp`. A program takes and returns all parts, laid end to end along the dimension named above; an argument that names none is the same for every part. Nothing has to cross between parts.
Inputs may be any that keep to these rules, and one draw needn't show every extreme that they name: `local_vals`: entries are 0 or between 0.1 and 1; a third or more of each tile's entries are nonzero. `remote_vals`: entries are 0 or between 0.1 and 1; a third or more of each tile's entries are nonzero. `local_cols`: the 8 entries of a block row differ. `remote_owner`: the 4 owners of one block row differ; among the tiles of the 16 block rows of one device, no owner is named more than 8 times.
All inputs are finite; a program needn't handle non-finite values. No bound on the sum of `remote_flag` on one device may be relied on, other than what follows from the above.
Results may differ from a plain program's by a relative error of at most 0.0075.
Values may be sent and summed in bfloat16 or wider, within the bound.
A program may use at most 128 MiB of HBM per device.

v0:
```python
import math

import jax
import jax.numpy as jnp
from jax import lax
from jax.sharding import PartitionSpec as P


def local(
    features,
    weight,
    grad_out,
    local_vals,
    local_cols,
    remote_vals,
    remote_owner,
    remote_index,
    remote_flag,
):
    block_size = local_vals.shape[2]
    blocks_dev = local_vals.shape[0]
    tiles_row = remote_vals.shape[1]
    feat = features.shape[1]
    row_count = lax.axis_size("row")
    slot_cap = max(2, 2 * blocks_dev * tiles_row // row_count)
    tile_count = blocks_dev * tiles_row
    node_count = blocks_dev * block_size
    xblocks = features.reshape(blocks_dev, block_size, feat)
    owners = remote_owner.reshape(-1)
    owner_hot = (owners[:, None] == jnp.arange(row_count, dtype=jnp.int32)[None, :]).astype(
        jnp.int32
    )
    ranks = jnp.sum((jnp.cumsum(owner_hot, axis=0) - owner_hot) * owner_hot, axis=1)
    slot_flat = owners * slot_cap + ranks
    request = (
        jnp.zeros((row_count * slot_cap,), jnp.int32).at[slot_flat].set(remote_index.reshape(-1))
    )
    request = request.reshape(row_count, slot_cap)
    masked = remote_vals * remote_flag[:, :, None, None].astype(jnp.bfloat16)
    tiles_flat = masked.reshape(tile_count, block_size, block_size)
    piece = lax.all_to_all(request, "row", split_axis=0, concat_axis=0, tiled=True)
    found = xblocks[piece]
    returned = lax.all_to_all(found, "row", split_axis=0, concat_axis=0, tiled=True)
    remote_x = returned.reshape(row_count * slot_cap, block_size, feat)[slot_flat]
    remote_sum = jnp.einsum(
        "tij,tjf->tif", tiles_flat, remote_x, preferred_element_type=jnp.float32
    )
    remote_sum = jnp.sum(remote_sum.reshape(blocks_dev, tiles_row, block_size, feat), axis=1)
    local_x = xblocks[local_cols]
    local_sum = jnp.einsum(
        "rlij,rljf->rif", local_vals, local_x, preferred_element_type=jnp.float32
    )
    agg = (
        (xblocks.astype(jnp.float32) + local_sum + remote_sum)
        .reshape(node_count, feat)
        .astype(jnp.bfloat16)
    )
    degree = jnp.sum(local_vals, axis=(1, 3), dtype=jnp.float32) + jnp.sum(
        masked, axis=(1, 3), dtype=jnp.float32
    )
    norm = lax.rsqrt(1.0 + degree.reshape(node_count))
    z_value = norm[:, None] * jnp.dot(agg, weight, preferred_element_type=jnp.float32)
    activated, pull = jax.vjp(jax.nn.gelu, z_value)
    hidden = activated.astype(jnp.bfloat16)
    grad_z = pull(grad_out.astype(jnp.float32))[0]
    scaled_grad = (norm[:, None] * grad_z).astype(jnp.bfloat16)
    weight_term = lax.dot_general(
        agg, scaled_grad, (((0,), (0,)), ((), ())), preferred_element_type=jnp.float32
    )
    total_nodes = node_count * row_count
    weight_grad = lax.psum(weight_term, "row") * (1.0 / math.sqrt(total_nodes))
    dagg = lax.dot_general(
        scaled_grad, weight, (((1,), (1,)), ((), ())), preferred_element_type=jnp.float32
    ).astype(jnp.bfloat16)
    dblocks = dagg.reshape(blocks_dev, block_size, feat)
    local_hot = (
        local_cols[:, :, None] == jnp.arange(blocks_dev, dtype=jnp.int32)[None, None, :]
    ).astype(jnp.float32)
    local_terms = jnp.einsum(
        "rlij,rif->rljf", local_vals, dblocks, preferred_element_type=jnp.float32
    )
    local_back = jnp.einsum("rlk,rljf->kjf", local_hot, local_terms)
    asked_hot = (
        piece[:, :, None] == jnp.arange(blocks_dev, dtype=jnp.int32)[None, None, :]
    ).astype(jnp.bfloat16)
    sender_terms = jnp.einsum(
        "rtij,rif->rtjf", masked, dblocks, preferred_element_type=jnp.float32
    ).astype(jnp.bfloat16)
    part_send = (
        jnp.zeros((row_count * slot_cap, block_size, feat), jnp.bfloat16)
        .at[slot_flat]
        .set(sender_terms.reshape(tile_count, block_size, feat))
    )
    received = lax.all_to_all(
        part_send.reshape(row_count, slot_cap, block_size, feat),
        "row",
        split_axis=0,
        concat_axis=0,
        tiled=True,
    )
    remote_back = jnp.einsum(
        "sck,scjf->kjf", asked_hot, received, preferred_element_type=jnp.float32
    )
    input_grad = (
        (dblocks.astype(jnp.float32) + local_back + remote_back)
        .reshape(node_count, feat)
        .astype(jnp.bfloat16)
    )
    return (hidden, input_grad, weight_grad)


def solution(mesh):
    return jax.shard_map(
        local,
        mesh=mesh,
        in_specs=(
            P(("grp", "row"), None),
            P(),
            P(("grp", "row"), None),
            P(("grp", "row"), None, None, None),
            P(("grp", "row"), None),
            P(("grp", "row"), None, None, None),
            P(("grp", "row"), None),
            P(("grp", "row"), None),
            P(("grp", "row"), None),
        ),
        out_specs=(P(("grp", "row"), None), P(("grp", "row"), None), P("grp", None)),
        check_vma=False,
    )
```

profile of v0, /device:TPU:0, one launch (start us, length us, event | category | flops | bytes accessed | tf_op | source)
XLA Modules:
  0.0 328.1 jit_solution(11325688523673309403)
XLA Ops:
  7.2 0.7 broadcast_multiply_fusion.2
  7.9 0.8 copy.37
  8.8 0.8 copy.38
  10.1 0.8 scatter_custom_fusion
  11.0 13.6 %all_to_all.22 = s32[16,1,8]{2,1,0:T(1,128)S(1)} all-to-all(s32[16,1,8]{2,1,0:T(1,128)S(1)} %bitcast.95), channel_id=1, replica_groups=mesh['grp'=2,'row'=16] {'row'}, dimensions={0} | all-to-all | bytes 1024 | tf_op jit(solution)/shard_map/all_to_all | solution.py:41
  24.9 4.1 %gather_fusion.1 = bf16[128,128,128]{2,1,0:T(8,128)(2,1)} fusion(bf16[16,128,128]{2,1,0:T(8,128)(2,1)} %bitcast.81, s32[1024]{0:T(1024)S(1)} %pad_clamp_fusion.1), kind=kCustom, calls=%fused_computation.1 | custom fusion | bytes 8389120 | tf_op jit(solution)/shard_map/gather | solution.py:42
  29.0 4.7 %all-to-all-start.1 = ((bf16[16,8,128,128]{3,2,1,0:T(8,128)(2,1)}), bf16[16,8,128,128]{3,2,1,0:T(8,128)(2,1)}, u32[]{:S(2)}, u32[]{:S(2)}) async-start(bf16[16,8,128,128]{3,2,1,0:T(8,128)(2,1)} %bitcast.87), calls=%async_computation.1 | async-start | bytes 8388608 | tf_op jit(solution)/shard_map/all_to_all | solution.py:43
  33.9 3.0 gather_fusion
  37.0 3.0 convert_reduce_fusion
  39.9 0.7 convert_reduce_fusion.1
  40.7 70.5 %all-to-all-done.1 = bf16[16,8,128,128]{3,2,1,0:T(8,128)(2,1)} async-done(((bf16[16,8,128,128]{3,2,1,0:T(8,128)(2,1)}), bf16[16,8,128,128]{3,2,1,0:T(8,128)(2,1)}, u32[]{:S(2)}, u32[]{:S(2)}) %all-to-all-start.1) | async-done | bytes 4194336 | tf_op jit(solution)/shard_map/all_to_all | solution.py:43
  111.2 4.4 %gather_fusion.2 = bf16[64,128,128]{2,1,0:T(8,128)(2,1)} fusion(bf16[128,128,128]{2,1,0:T(8,128)(2,1)} %bitcast.12, s32[1024]{0:T(1024)S(1)} %pad_clamp_fusion), kind=kCustom, calls=%fused_computation.2 | custom fusion | bytes 4194560 | tf_op jit(solution)/shard_map/gather | solution.py:44
  115.6 2.5 bitcast_reduce_fusion
  118.1 0.3 copy-done.2
  118.4 3.6 %fusion.22 = bf16[16,128,128]{2,1,0:T(8,128)(2,1)S(1)} fusion(f32[16,128,128]{2,1,0:T(8,128)S(1)} %bitcast_reduce_fusion, bf16[16,8,128,128]{3,2,1,0:T(8,128)(2,1)S(1)} %copy-done.2, bf16[16,8,128,128]{3,2,1,0:T(8,128)(2,1)} %bitcast.84, bf16[16,128,128]{2,1,0:T(8,128)(2,1)S(1)} %bitcast.83), kind=kOutput, calls=%fused_computation.37 | convolution fusion | flops 537919488 | bytes 10485760 | tf_op jit(solution)/shard_map/rlij,rljf->rif/dot_general | solution.py:50
  122.0 2.9 fusion.5
  124.9 1.1 copy-done.4
  126.0 0.4 convolution_convert_fusion
  126.4 2.1 convolution_convert_fusion.1
  128.6 3.0 broadcast_in_dim.8
  131.6 8.7 %scatter_fusion = bf16[128,128,128]{2,1,0:T(8,128)(2,1)} fusion(bf16[128,128,128]{2,1,0:T(8,128)(2,1)} %broadcast_in_dim.8, s32[64]{0:T(128)S(1)} %fusion.33, bf16[64,128,128]{2,1,0:T(8,128)(2,1)S(1)} %bitcast.91), kind=kCustom, calls=%fused_computation.4 | custom fusion | bytes 6291712 | tf_op jit(solution)/shard_map/scatter | solution.py:92
  140.3 7.7 %copy.47 = bf16[16,8,128,128]{3,1,2,0:T(8,128)(2,1)} copy(bf16[16,8,128,128]{3,2,1,0:T(8,128)(2,1)} %bitcast.85) | data formatting | bytes 8388608 | tf_op jit(solution)/shard_map/reshape | solution.py:95
  147.9 19.7 %all-to-all-start.2 = ((bf16[16,8,128,128]{3,1,2,0:T(8,128)(2,1)}), bf16[16,8,128,128]{3,1,2,0:T(8,128)(2,1)}, u32[]{:S(2)}, u32[]{:S(2)}) async-start(bf16[16,8,128,128]{3,1,2,0:T(8,128)(2,1)} %copy.47), calls=%async_computation.2 | async-start | bytes 8388608 | tf_op jit(solution)/shard_map/all_to_all | solution.py:94
  167.7 0.2 all-reduce.2.cloned.1.call-start
  167.9 1.0 fusion.36
  168.9 5.5 %convolution_bitcast_fusion = bf16[16,8,128,128]{2,3,1,0:T(8,128)(2,1)} fusion(bf16[16,128,128,1]{2,1,3,0:T(8,128)(2,1)S(1)} %bitcast.89, bf16[16,8,128,128]{3,2,1,0:T(8,128)(2,1)} %param.12), kind=kOutput, calls=%fused_computation.10 | convolution fusion | flops 536870912 | bytes 8912896 | tf_op jit(solution)/shard_map/rlij,rif->rljf/dot_general | solution.py:79
  174.4 6.8 %copy.44 = bf16[16,8,128,128]{3,0,1,2:T(8,128)(2,1)} copy(bf16[16,8,128,128]{2,3,1,0:T(8,128)(2,1)} %convolution_bitcast_fusion) | data formatting | bytes 8388608 | tf_op jit(solution)/shard_map/rlij,rif->rljf/dot_general | solution.py:79
  181.2 3.5 %fusion.21 = f32[16,128,128]{2,0,1:T(8,128)S(1)} fusion(bf16[16,8,128,128]{3,0,1,2:T(8,128)(2,1)} %copy.44, bf16[16,128,128]{2,1,0:T(8,128)(2,1)S(1)} %bitcast.90, s32[16,8]{0,1:T(8,128)S(1)} %copy-done.7), kind=kOutput, calls=%fused_computation.36 | convolution fusion | flops 67635200 | bytes 5767680 | tf_op jit(solution)/shard_map/rlk,rljf->kjf/dot_general | solution.py:82
  184.7 129.4 %all-reduce.2.cloned.1.call-done = f32[128,256]{1,0:T(8,128)} async-done(((f32[128,256]{1,0:T(8,128)}), f32[128,256]{1,0:T(8,128)}) %all-reduce.2.cloned.1.call-update) | async-done | bytes 131088 | tf_op jit(solution)/shard_map/psum | solution.py:71
  314.1 1.6 broadcast_multiply_fusion.1
  315.7 4.6 %fusion.23 = bf16[16,128,128]{2,0,1:T(8,128)(2,1)S(1)} fusion(f32[16,128,128]{2,0,1:T(8,128)S(1)} %fusion.21, bf16[16,8,128,128]{3,1,2,0:T(8,128)(2,1)} %all-to-all-done.2, s32[16,8]{0,1:T(8,128)S(1)} %bitcast.96), kind=kOutput, calls=%fused_computation.38 | convolution fusion | flops 67635200 | bytes 5767680 | tf_op jit(solution)/shard_map/sck,scjf->kjf/dot_general | solution.py:101
  320.3 0.9 copy.49
  (42 shorter events, 1.4 us)
Async XLA Ops:
  7.2 114.8 %copy-start = (bf16[128,256]{1,0:T(8,128)(2,1)S(1)}, bf16[128,256]{1,0:T(8,128)(2,1)}, u32[]{:S(2)}) copy-start(bf16[128,256]{1,0:T(8,128)(2,1)} %param.10) | copy-start | bytes 196612
  29.0 4.7 %copy-start.8 = (s32[16,4]{0,1:T(4,128)S(1)}, s32[16,4]{0,1:T(4,128)}, u32[]{:S(2)}) copy-start(s32[16,4]{0,1:T(4,128)} %param.17) | copy-start | bytes 772
  29.0 4.8 %copy-start.7 = (s32[16,8]{0,1:T(8,128)S(1)}, s32[16,8]{0,1:T(8,128)}, u32[]{:S(2)}) copy-start(s32[16,8]{0,1:T(8,128)} %param.13) | copy-start | bytes 1540
  29.0 5.0 %copy-start.1 = (bf16[2048,128]{1,0:T(8,128)(2,1)S(1)}, bf16[2048,128]{1,0:T(8,128)(2,1)}, u32[]{:S(2)}) copy-start(bf16[2048,128]{1,0:T(8,128)(2,1)} %param.9) | copy-start | bytes 1572868
  29.0 82.3 %all-to-all-start.1 = ((bf16[16,8,128,128]{3,2,1,0:T(8,128)(2,1)}), bf16[16,8,128,128]{3,2,1,0:T(8,128)(2,1)}, u32[]{:S(2)}, u32[]{:S(2)}) async-start(bf16[16,8,128,128]{3,2,1,0:T(8,128)(2,1)} %bitcast.87), calls=%async_computation.1 | async-start | bytes 8388608 | tf_op jit(solution)/shard_map/all_to_all | solution.py:43
  37.0 3.0 copy-start.6
  115.6 2.8 copy-start.2
  118.4 3.6 %copy-start.9 = (bf16[2048,256]{1,0:T(8,128)(2,1)S(1)}, bf16[2048,256]{1,0:T(8,128)(2,1)}, u32[]{:S(2)}) copy-start(bf16[2048,256]{1,0:T(8,128)(2,1)} %param.11) | copy-start | bytes 3145732
  124.9 1.1 copy-start.4
  128.6 3.0 copy-start.3
  147.9 20.0 %copy-start.5 = (bf16[2048,256]{1,0:T(8,128)(2,1)S(1)}, bf16[2048,256]{1,0:T(8,128)(2,1)}, u32[]{:S(2)}) copy-start(bf16[2048,256]{1,0:T(8,128)(2,1)} %copy-done.4) | copy-start | bytes 3145732
  147.9 167.8 %all-to-all-start.2 = ((bf16[16,8,128,128]{3,1,2,0:T(8,128)(2,1)}), bf16[16,8,128,128]{3,1,2,0:T(8,128)(2,1)}, u32[]{:S(2)}, u32[]{:S(2)}) async-start(bf16[16,8,128,128]{3,1,2,0:T(8,128)(2,1)} %copy.47), calls=%async_computation.2 | async-start | bytes 8388608 | tf_op jit(solution)/shard_map/all_to_all | solution.py:94
  167.7 146.5 %all-reduce.2.cloned.1.call-start = ((), (), s32[]{:S(2)}) async-start(), calls=%async_computation.3 | async-start | bytes 262144 | tf_op jit(solution)/shard_map/psum | solution.py:71
Sparse Core Ops, SparseCore 0:
  172.5 141.5 all-reduce.1
where the time goes:
time: 330 us; the launch traced here: 328 us
  waiting for transfers between devices  200 us (61%)
  local copies, waits for them, and re-layouts  43.2 us (13%)
  matrix products  26.1 us (8%)
  starting transfers between devices  24.6 us (7%)
  between operations  14.2 us (4%)
  blocking collectives  13.6 us (4%)
  other arithmetic  6.39 us (2%)
    psum x1, waiting for transfers between devices, local(): weight_grad = lax.psum(weight_term, 'row') * (1.0 / math.sqrt(total_nodes))  129 us
    all_to_all x1, waiting for transfers between devices, local(): lax.all_to_all(found, 'row', split_axis=0, concat_axis=0, tiled=True)  70.5 us
    all_to_all x1, starting transfers between devices, local(): lax.all_to_all(part_send.reshape(row_count, slot_cap, block_size, feat),...  19.7 us
    all_to_all x1, blocking collectives, local(): lax.all_to_all(request, 'row', split_axis=0, concat_axis=0, tiled=True)  13.6 us
    scatter x1, local copies, waits for them, and re-layouts, local(): part_send = jnp.zeros((row_count * slot_cap, block_size, feat), jnp.bfloa...  8.68 us
    reshape x1, local copies, waits for them, and re-layouts, local(): part_send.reshape(row_count, slot_cap, block_size, feat)  7.66 us
    dot_general x1, local copies, waits for them, and re-layouts, local(): jnp.einsum('rlij,rif->rljf', local_vals, dblocks, preferred_element_type=...  6.8 us
  transfers between devices with their start and end apart: 3, of which 2 were waited for; matrix products, arithmetic and copies ran while one was open for 8% of the time, Pallas kernels for 0%

commit v1 on v0

--- a/solution.py
+++ b/solution.py
@@ -1,12 +1,15 @@
+import functools
 import math
 
 import jax
 import jax.numpy as jnp
 from jax import lax
+from jax.experimental import pallas as pl
+from jax.experimental.pallas import tpu as pltpu
 from jax.sharding import PartitionSpec as P
 
 
-def local(
+def slotted(
     features,
     weight,
     grad_out,
@@ -109,9 +112,528 @@
     return (hidden, input_grad, weight_grad)
 
 
+MESH = pl.DeviceIdType.MESH
+RIGHT, LEFT, ACROSS, SIBLING = 0, 1, 2, 3
+PIECES = 4
+
+
+def place():
+    me = lax.axis_index("row")
+    core = lax.rem(me, 2)
+    yy = lax.rem(lax.div(me, 2), 2)
+    zz = lax.div(me, 4)
+    return me, core, yy, zz, me + 1 - 2 * core, me + 2 - 4 * yy
+
+
+def signal(barrier, device):
+    pl.semaphore_signal(barrier, inc=1, device_id={"row": device}, device_id_type=MESH)
+
+
+def gather_kernel(zs, x_ref, out_ref, own_sem, send_sem, recv_sem):
+    me, core, yy, zz, sib, ynb = place()
+    rows = x_ref.shape[0] // PIECES
+    has_left, has_right = zz > 0, zz < zs - 1
+
+    barrier = pltpu.get_barrier_semaphore()
+    signal(barrier, sib)
+    signal(barrier, ynb)
+    pl.when(has_left)(lambda: signal(barrier, me - 4))
+    pl.when(has_right)(lambda: signal(barrier, me + 4))
+    pl.semaphore_wait(barrier, 2 + has_left.astype(jnp.int32) + has_right.astype(jnp.int32))
+
+    own = pltpu.make_async_copy(x_ref, out_ref.at[me], own_sem)
+    own.start()
+
+    def copy(kind, shard, j, device, mine=False):
+        zt = lax.div(shard, 4)
+        slot = zt if kind != SIBLING else zt + zs * lax.rem(lax.div(shard, 2), 2)
+        cut = pl.ds(pl.multiple_of(j * rows, rows), rows)
+        there = out_ref.at[shard, cut]
+        return pltpu.make_async_remote_copy(
+            src_ref=x_ref.at[cut] if mine else there,
+            dst_ref=there,
+            send_sem=send_sem.at[kind * zs + slot, j],
+            recv_sem=recv_sem.at[shard, j],
+            device_id={"row": device},
+            device_id_type=MESH,
+        )
+
+    def each(body):
+        lax.fori_loop(0, PIECES, lambda j, c: (body(j), c)[1], 0)
+
+    def own_sends(act):
+        def body(j):
+            pl.when(has_right)(lambda: act(copy(RIGHT, me, j, me + 4, True)))
+            pl.when(has_left)(lambda: act(copy(LEFT, me, j, me - 4, True)))
+            act(copy(ACROSS, me, j, ynb, True))
+            act(copy(SIBLING, me, j, sib, True))
+
+        each(body)
+
+    def along(act, wait):
+        for k in range(1, zs):
+            for sign in (-1, 1):
+                shard = me + sign * 4 * k
+                onward = has_right if sign < 0 else has_left
+                kind = RIGHT if sign < 0 else LEFT
+
+                def body(j, shard=shard, onward=onward, kind=kind, sign=sign):
+                    if wait:
+                        copy(SIBLING, shard, j, sib).wait_recv()
+                    pl.when(onward)(lambda: act(copy(kind, shard, j, me - sign * 4)))
+                    act(copy(ACROSS, shard, j, ynb))
+                    act(copy(SIBLING, shard, j, sib))
+
+                pl.when(zz >= k if sign < 0 else zz + k < zs)(functools.partial(each, body))
+
+    def across(act, wait):
+        for k in range(zs):
+            for sign in (-1, 1):
+                if k == 0 and sign == 1:
+                    continue
+                shard = ynb + sign * 4 * k
+
+                def body(j, shard=shard):
+                    if wait:
+                        copy(SIBLING, shard, j, sib).wait_recv()
+                    act(copy(SIBLING, shard, j, sib))
+
+                pl.when(zz >= k if sign < 0 else zz + k < zs)(functools.partial(each, body))
+
+    start = lambda c: c.start()
+    finish = lambda c: c.wait_send()
+    own_sends(start)
+    along(start, True)
+    across(start, True)
+    for q in range(2 * zs):
+        shard = 2 * q + 1 - core
+        each(lambda j, shard=shard: copy(SIBLING, shard, j, sib).wait_recv())
+    own.wait()
+    own_sends(finish)
+    along(finish, False)
+    across(finish, False)
+
+
+def gather(x, row_count):
+    zs = row_count // 4
+    return pl.pallas_call(
+        functools.partial(gather_kernel, zs),
+        out_shape=jax.ShapeDtypeStruct((row_count,) + x.shape, x.dtype),
+        in_specs=[pl.BlockSpec(memory_space=pl.ANY)],
+        out_specs=pl.BlockSpec(memory_space=pl.ANY),
+        scratch_shapes=[
+            pltpu.SemaphoreType.DMA,
+            pltpu.SemaphoreType.DMA((5 * zs, PIECES)),
+            pltpu.SemaphoreType.DMA((row_count, PIECES)),
+        ],
+        compiler_params=pltpu.CompilerParams(collective_id=0, has_side_effects=True),
+        name="gather_features",
+    )(x)
+
+
+def layer_kernel(
+    tiles_row,
+    lcol,
+    rcol,
+    flag,
+    x_ref,
+    *refs,
+):
+    far = refs[:tiles_row]
+    weight_ref, grad_ref, lv_ref, rv_ref, hidden_ref, part_ref, base_ref, wg_ref = refs[tiles_row:]
+    r = pl.program_id(0)
+    lb = lv_ref.shape[1]
+    block, feat = lv_ref.shape[2], x_ref.shape[2]
+    f32, bf16 = jnp.float32, jnp.bfloat16
+
+    @pl.when(r == 0)
+    def _():
+        base_ref[...] = jnp.zeros_like(base_ref)
+        wg_ref[...] = jnp.zeros_like(wg_ref)
+
+        def clear(i, c):
+            part_ref[i] = jnp.zeros(part_ref.shape[1:], bf16)
+            return c
+
+        lax.fori_loop(0, part_ref.shape[0], clear, 0)
+
+    ones = jnp.ones((block, feat), bf16)
+    flags = [flag[r * tiles_row + t].astype(f32) for t in range(tiles_row)]
+    tiles = [lv_ref[0, l] for l in range(lb)] + [rv_ref[0, t] for t in range(tiles_row)]
+    blocks = [jnp.concatenate([x_ref[lcol[r * lb + l]], ones], axis=1) for l in range(lb)]
+    for t in range(tiles_row):
+        seen = jnp.concatenate([far[t][0], ones], axis=1)
+        blocks.append((seen.astype(f32) * flags[t]).astype(bf16))
+    total = jnp.dot(
+        jnp.concatenate(tiles, axis=1),
+        jnp.concatenate(blocks, axis=0),
+        preferred_element_type=f32,
+    )
+    agg = (x_ref[r].astype(f32) + total[:, :feat]).astype(bf16)
+    norm = lax.rsqrt(1.0 + total[:, feat:])
+    hid = weight_ref.shape[1]
+    norm = jnp.concatenate([norm] * (hid // feat), axis=1)
+    v = norm * jnp.dot(agg, weight_ref[...], preferred_element_type=f32)
+    scale = math.sqrt(2.0 / math.pi)
+    square = v * v
+    t = jnp.tanh(scale * (v + 0.044715 * (square * v)))
+    half = 0.5 * (1.0 + t)
+    hidden_ref[...] = (v * half).astype(bf16)
+    slope = half + (0.5 * scale) * v * (1.0 - t * t) * (1.0 + (3 * 0.044715) * square)
+    gs = (norm * (grad_ref[...].astype(f32) * slope)).astype(bf16)
+    wg_ref[...] += lax.dot_general(agg, gs, (((0,), (0,)), ((), ())), preferred_element_type=f32)
+    dagg = lax.dot_general(
+        weight_ref[...], gs, (((1,), (1,)), ((), ())), preferred_element_type=f32
+    ).astype(bf16)
+    base_ref[r] += dagg.astype(f32)
+    terms = jnp.dot(dagg, jnp.concatenate(tiles, axis=1), preferred_element_type=f32)
+    for l in range(lb):
+        base_ref[lcol[r * lb + l]] += terms[:, l * block : (l + 1) * block]
+    for t in range(tiles_row):
+        at = rcol[r * tiles_row + t]
+        term = terms[:, (lb + t) * block : (lb + t + 1) * block] * flags[t]
+        part_ref[at] = (part_ref[at].astype(f32) + term).astype(bf16)
+
+
+def layer(x, seen, weight, grad_out, local_vals, remote_vals, lcol, rcol, flag):
+    blocks_dev, lb, block, _ = local_vals.shape
+    tiles_row = remote_vals.shape[1]
+    feat, hid = weight.shape
+    whole = lambda *shape: pl.BlockSpec(shape, lambda r, *_: (0,) * len(shape))
+    far = [
+        pl.BlockSpec((1, block, feat), lambda r, lc, rc, fl, t=t: (rc[r * tiles_row + t], 0, 0))
+        for t in range(tiles_row)
+    ]
+    return pl.pallas_call(
+        functools.partial(layer_kernel, tiles_row),
+        grid_spec=pltpu.PrefetchScalarGridSpec(
+            num_scalar_prefetch=3,
+            grid=(blocks_dev,),
+            in_specs=[whole(blocks_dev, block, feat)]
+            + far
+            + [
+                whole(feat, hid),
+                pl.BlockSpec((block, hid), lambda r, *_: (r, 0)),
+                pl.BlockSpec((1, lb, block, block), lambda r, *_: (r, 0, 0, 0)),
+                pl.BlockSpec((1, tiles_row, block, block), lambda r, *_: (r, 0, 0, 0)),
+            ],
+            out_specs=[
+                pl.BlockSpec((block, hid), lambda r, *_: (r, 0)),
+                whole(seen.shape[0], feat, block),
+                whole(blocks_dev, feat, block),
+                whole(feat, hid),
+            ],
+        ),
+        out_shape=[
+            jax.ShapeDtypeStruct((blocks_dev * block, hid), jnp.bfloat16),
+            jax.ShapeDtypeStruct((seen.shape[0], feat, block), jnp.bfloat16),
+            jax.ShapeDtypeStruct((blocks_dev, feat, block), jnp.float32),
+            jax.ShapeDtypeStruct((feat, hid), jnp.float32),
+        ],
+        compiler_params=pltpu.CompilerParams(
+            dimension_semantics=("arbitrary",), vmem_limit_bytes=48 << 20
+        ),
+        name="layer",
+    )(lcol, rcol, flag, x, *([seen] * tiles_row), weight, grad_out, local_vals, remote_vals)
+
+
+def scatter_kernel(
+    zs,
+    part_ref,
+    base_ref,
+    w_ref,
+    out_ref,
+    wout_ref,
+    mine,
+    from_core,
+    from_y,
+    from_z,
+    held,
+    base_sum,
+    w_in,
+    w_sum,
+    load_sem,
+    send_sem,
+    core_sem,
+    y_sem,
+    z_sem,
+    w_send,
+    w_recv,
+):
+    me, core, yy, zz, sib, ynb = place()
+    rows = part_ref.shape[1] // PIECES
+    has_left, has_right = zz > 0, zz < zs - 1
+    f32, bf16 = jnp.float32, jnp.bfloat16
+    near = me + 4 * (1 - 2 * lax.rem(zz, 2))
+    apart = me + 8 * (1 - 2 * lax.div(zz, 2))
+
+    def load(zt, yt):
+        q = yt * zs + zt
+        return pltpu.make_async_copy(
+            part_ref.at[zt * 4 + yt * 2 + core], mine.at[q], load_sem.at[q]
+        )
+
+    for yt in range(2):
+        for zt in range(zs):
+            load(zt, yt).start()
+
+    barrier = pltpu.get_barrier_semaphore()
+    signal(barrier, sib)
+    signal(barrier, ynb)
+    signal(barrier, apart)
+    pl.when(has_left)(lambda: signal(barrier, me - 4))
+    pl.when(has_right)(lambda: signal(barrier, me + 4))
+    pl.semaphore_wait(barrier, 3 + has_left.astype(jnp.int32) + has_right.astype(jnp.int32))
+
+    def each(body):
+        lax.fori_loop(0, PIECES, lambda j, c: (body(j), c)[1], 0)
+
+    def cut(j):
+        return pl.ds(pl.multiple_of(j * rows, rows), rows)
+
+    def remote(src, dst, send, recv, device):
+        return pltpu.make_async_remote_copy(
+            src_ref=src,
+            dst_ref=dst,
+            send_sem=send,
+            recv_sem=recv,
+            device_id={"row": device},
+            device_id_type=MESH,
+        )
+
+    wrows = w_ref.shape[0] // 2
+    kept = pl.ds(pl.multiple_of(core * wrows, wrows), wrows)
+    given = pl.ds(pl.multiple_of((1 - core) * wrows, wrows), wrows)
+    w_steps = [
+        remote(w_ref.at[given], w_in.at[0], w_send.at[0], w_recv.at[0], sib),
+        remote(w_sum.at[0], w_in.at[1], w_send.at[1], w_recv.at[1], ynb),
+        remote(w_sum.at[1], w_in.at[2], w_send.at[2], w_recv.at[2], near),
+        remote(w_sum.at[2], w_in.at[3], w_send.at[3], w_recv.at[3], apart),
+    ]
+    w_last = remote(wout_ref.at[kept], wout_ref.at[kept], w_send.at[4], w_recv.at[4], sib)
+    w_back = remote(wout_ref.at[given], wout_ref.at[given], w_send.at[4], w_recv.at[4], sib)
+
+    def w_go(step):
+        w_steps[step].wait_recv()
+        held_so_far = w_ref[kept] if step == 0 else w_sum[step - 1]
+        total = held_so_far + w_in[step]
+        if step < 3:
+            w_sum[step] = total
+            w_steps[step + 1].start()
+        else:
+            wout_ref[kept] = total
+            w_last.start()
+
+    w_steps[0].start()
+
+    def valid(sign, d):
+        return zz >= d if sign < 0 else zz + d < zs
+
+    def order(least):
+        for d in range(zs - 1, least - 1, -1):
+            for sign in (1, -1) if d else (1,):
+                yield d, sign
+
+    def to_core(zt, yt, j):
+        return remote(
+            part_ref.at[zt * 4 + yt * 2 + 1 - core, cut(j)],
+            from_core.at[yt * zs + zt, cut(j)],
+            send_sem.at[yt * zs + zt, j],
+            core_sem.at[yt * zs + zt, j],
+            sib,
+        )
+
+    def to_y(zt, j):
+        return remote(
+            held.at[(1 - yy) * zs + zt, cut(j)],
+            from_y.at[zt, cut(j)],
+            send_sem.at[2 * zs + zt, j],
+            y_sem.at[zt, j],
+            ynb,
+        )
+
+    def to_z(zt, way, j, device):
+        return remote(
+            held.at[yy * zs + zt, cut(j)],
+            from_z.at[way, zt, cut(j)],
+            send_sem.at[3 * zs + zt, j],
+            z_sem.at[way, zt, j],
+            device,
+        )
+
+    for yt in (1 - yy, yy):
+        for d, sign in order(0):
+            zt = zz + sign * d
+            pl.when(valid(sign, d))(
+                functools.partial(each, lambda j, zt=zt, yt=yt: to_core(zt, yt, j).start())
+            )
+
+    w_go(0)
+    step = 1
+    for d, sign in order(0):
+        zt = zz + sign * d
+
+        @pl.when(valid(sign, d))
+        def _(zt=zt):
+            q = (1 - yy) * zs + zt
+            load(zt, 1 - yy).wait()
+
+            def body(j):
+                to_core(zt, 1 - yy, j).wait_recv()
+                total = mine[q, cut(j)].astype(f32) + from_core[q, cut(j)].astype(f32)
+                held[q, cut(j)] = total.astype(bf16)
+                to_y(zt, j).start()
+
+            each(body)
+
+    def summed(zt, j):
+        q = yy * zs + zt
+        to_core(zt, yy, j).wait_recv()
+        to_y(zt, j).wait_recv()
+        total = mine[q, cut(j)].astype(f32) + from_core[q, cut(j)].astype(f32)
+        return total + from_y[zt, cut(j)].astype(f32)
+
+    w_go(1)
+    step = 2
+    for d, sign in order(1):
+        zt = zz + sign * d
+        way = 0 if sign > 0 else 1
+        behind = has_left if sign > 0 else has_right
+
+        @pl.when(valid(sign, d))
+        def _(zt=zt, way=way, behind=behind, sign=sign):
+            load(zt, yy).wait()
+
+            def body(j):
+                total = summed(zt, j)
+                q = yy * zs + zt
+
+                @pl.when(behind)
+                def _():
+                    to_z(zt, way, j, me + sign * 4).wait_recv()
+                    held[q, cut(j)] = (total + from_z[way, zt, cut(j)].astype(f32)).astype(bf16)
+
+                @pl.when(jnp.logical_not(behind))
+                def _():
+                    held[q, cut(j)] = total.astype(bf16)
+
+                to_z(zt, way, j, me + sign * 4).start()
+
+            each(body)
+
+        if sign < 0 and step < 4:
+            w_go(step)
+            step += 1
+
+    load(zz, yy).wait()
+
+    def last(j):
+        base_sum[cut(j)] = base_ref[cut(j)] + summed(zz, j)
+
+        @pl.when(has_left)
+        def _():
+            to_z(zz, 0, j, sib).wait_recv()
+            base_sum[cut(j)] += from_z[0, zz, cut(j)].astype(f32)
+
+        @pl.when(has_right)
+        def _():
+            to_z(zz, 1, j, sib).wait_recv()
+            base_sum[cut(j)] += from_z[1, zz, cut(j)].astype(f32)
+
+        out_ref[cut(j)] = base_sum[cut(j)].astype(bf16)
+
+    each(last)
+
+    w_back.wait_recv()
+    for c in w_steps:
+        c.wait_send()
+    w_last.wait_send()
+    for zt in range(zs):
+        each(lambda j, zt=zt: to_core(zt, 0, j).wait_send())
+        each(lambda j, zt=zt: to_core(zt, 1, j).wait_send())
+        each(lambda j, zt=zt: to_y(zt, j).wait_send())
+        pl.when(zz != zt)(
+            functools.partial(each, lambda j, zt=zt: to_z(zt, 0, j, sib).wait_send())
+        )
+
+
+def scatter(part, base, wterm, row_count):
+    zs = row_count // 4
+    nodes, feat = base.shape
+    vmem = pl.BlockSpec(memory_space=pltpu.VMEM)
+    dma = pltpu.SemaphoreType.DMA
+    shard = lambda *lead: pltpu.VMEM(lead + (nodes, feat), jnp.bfloat16)
+    wshape = (wterm.shape[0] // 2, wterm.shape[1])
+    return pl.pallas_call(
+        functools.partial(scatter_kernel, zs),
+        out_shape=[
+            jax.ShapeDtypeStruct((nodes, feat), jnp.bfloat16),
+            jax.ShapeDtypeStruct(wterm.shape, jnp.float32),
+        ],
+        in_specs=[pl.BlockSpec(memory_space=pl.ANY), vmem, vmem],
+        out_specs=[vmem, vmem],
+        scratch_shapes=[
+            shard(2 * zs),
+            shard(2 * zs),
+            shard(zs),
+            shard(2, zs),
+            shard(2 * zs),
+            pltpu.VMEM((nodes, feat), jnp.float32),
+            pltpu.VMEM((4,) + wshape, jnp.float32),
+            pltpu.VMEM((3,) + wshape, jnp.float32),
+            dma((2 * zs,)),
+            dma((4 * zs, PIECES)),
+            dma((2 * zs, PIECES)),
+            dma((zs, PIECES)),
+            dma((2, zs, PIECES)),
+            dma((5,)),
+            dma((5,)),
+        ],
+        compiler_params=pltpu.CompilerParams(
+            collective_id=1, has_side_effects=True, vmem_limit_bytes=48 << 20
+        ),
+        name="scatter_gradient",
+    )(part, base, wterm)
+
+
+def planned(
+    features,
+    weight,
+    grad_out,
+    local_vals,
+    local_cols,
+    remote_vals,
+    remote_owner,
+    remote_index,
+    remote_flag,
+):
+    blocks_dev, _, block, _ = local_vals.shape
+    nodes, feat = features.shape
+    row_count = lax.axis_size("row")
+    seen = gather(features, row_count).reshape(row_count * blocks_dev, block, feat)
+    rcol = (remote_owner * blocks_dev + remote_index).reshape(-1)
+    hidden, part, base, wterm = layer(
+        features.reshape(blocks_dev, block, feat),
+        seen,
+        weight,
+        grad_out,
+        local_vals,
+        remote_vals,
+        local_cols.reshape(-1),
+        rcol,
+        remote_flag.reshape(-1),
+    )
+    back, wsum = scatter(
+        part.reshape(row_count, nodes, feat), base.reshape(nodes, feat), wterm, row_count
+    )
+    input_grad = jnp.swapaxes(back.reshape(blocks_dev, feat, block), 1, 2).reshape(nodes, feat)
+    weight_grad = wsum * (1.0 / math.sqrt(nodes * row_count))
+    return hidden, input_grad, weight_grad
+
+
 def solution(mesh):
     return jax.shard_map(
-        local,
+        planned if mesh.shape["row"] == 16 else slotted,
         mesh=mesh,
         in_specs=(
             P(("grp", "row"), None),

time: 330 us -> 137 us (0.42)
  waiting for transfers between devices: 200 us -> 0 us
  Pallas kernels: 0 us -> 130 us
  local copies, waits for them, and re-layouts: 43.2 us -> 4.11 us
  matrix products: 26.1 us -> 0 us
  starting transfers between devices: 24.6 us -> 0 us
  blocking collectives: 13.6 us -> 0 us
  between operations: 14.2 us -> 0.71 us
  other arithmetic: 6.39 us -> 1.52 us
    pallas_call x0 -> x3, Pallas kernels: none -> 130 us  [the longest x1 53.6 us: scatter(): pl.pallas_call(functools.partial(scatter_kernel, zs), out_shape=[jax.Shap...]
    psum x1 -> x0, waiting for transfers between devices: 129 us -> none  [local(): weight_grad = lax.psum(weight_term, 'row') * (1.0 / math.sqrt(total_nodes))]
    all_to_all x2 -> x0, waiting for transfers between devices: 70.5 us -> none  [the longest x1 70.5 us: local(): lax.all_to_all(found, 'row', split_axis=0, concat_axis=0, tiled=True)]
    dot_general x9 -> x0, matrix products: 26.1 us -> none  [the longest x1 5.46 us: local(): jnp.einsum('rlij,rif->rljf', local_vals, dblocks, preferred_element_type=...]
    all_to_all x2 -> x0, starting transfers between devices: 24.4 us -> none  [the longest x1 19.7 us: local(): lax.all_to_all(part_send.reshape(row_count, slot_cap, block_size, feat),...]
    all_to_all x1 -> x0, blocking collectives: 13.6 us -> none  [local(): lax.all_to_all(request, 'row', split_axis=0, concat_axis=0, tiled=True)]
    gather x3 -> x0, local copies, waits for them, and re-layouts: 11.5 us -> none  [the longest x1 4.39 us: local(): returned.reshape(row_count * slot_cap, block_size, feat)[slot_flat]]
    scatter x2 -> x0, local copies, waits for them, and re-layouts: 9.46 us -> none  [the longest x1 8.68 us: local(): part_send = jnp.zeros((row_count * slot_cap, block_size, feat), jnp.bfloa...]
  transfers between devices with their start and end apart: 3 -> 0, of which waited for: 2 -> 0; matrix products, arithmetic and copies ran while one was open for 8% -> 0% of each run, Pallas kernels for 0% -> 0%
where the time goes in v1:
time: 137 us
  Pallas kernels  130 us (95%)
  local copies, waits for them, and re-layouts  4.11 us (3%)
  other arithmetic  1.52 us (1%)
    pallas_call x1, Pallas kernels, scatter(): pl.pallas_call(functools.partial(scatter_kernel, zs), out_shape=[jax.Shap...  53.6 us
    pallas_call x1, Pallas kernels, gather(): pl.pallas_call(functools.partial(gather_kernel, zs), out_shape=jax.ShapeD...  52.9 us
    pallas_call x1, Pallas kernels, layer(): pl.pallas_call(functools.partial(layer_kernel, tiles_row), grid_spec=pltp...  23.7 us
    unnamed x10, local copies, waits for them, and re-layouts  2.76 us

profile of v1, /device:TPU:0, one launch (start us, length us, event | category | flops | bytes accessed | tf_op | source)
XLA Modules:
  0.0 136.6 jit_solution(13966995025669846945)
XLA Ops:
  0.6 0.0 copy-start
  0.6 0.0 copy-start.1
  0.7 0.0 copy-start.3
  0.7 0.9 multiply_add_fusion
  1.5 0.1 copy.17
  1.6 0.1 reshape.34.rcol
  1.7 0.8 copy.16
  2.5 0.1 reshape.33.lcol
  2.5 0.8 copy.18
  3.3 0.1 reshape.35.flag
  3.4 52.9 %gather_features.1 = bf16[16,2048,128]{2,1,0:T(8,128)(2,1)} custom-call(bf16[2048,128]{1,0:T(8,128)(2,1)} %x_ref.1), custom_call_target="tpu_custom_call" | custom-call | tf_op jit(solution)/shard_map/gather_features/pallas_call | solution.py:219
  56.3 0.0 copy-done
  56.3 0.0 copy-done.1
  56.3 0.0 copy-done.3
  56.4 0.0 copy-start.2
  56.4 1.2 copy-done.2
  57.6 23.7 %layer.1 = (bf16[2048,256]{1,0:T(8,128)(2,1)}, bf16[256,128,128]{2,1,0:T(8,128)(2,1)}, f32[16,128,128]{2,1,0:T(8,128)S(1)}, f32[128,256]{1,0:T(8,128)S(1)}) custom-call(s32[128]{0:T(128)S(1)} %reshape.33.lcol, s32[64]{0:T(128)S(1)} %reshape.34.rcol, s32[64]{0:T(128)S(1)} %reshape.35.flag, bf16[16,128,128]{2,1,0:T(8,128)(2,1)S(1)} %bitcast.8, ...), custom_call_target="tpu_custom_call" | custom-call | tf_op jit(solution)/shard_map/layer/pallas_call | solution.py:307
  81.2 53.6 %scatter_gradient.1 = (bf16[2048,128]{1,0:T(8,128)(2,1)S(1)}, f32[128,256]{1,0:T(8,128)S(1)}) custom-call(bf16[16,2048,128]{2,1,0:T(8,128)(2,1)} %bitcast.15, f32[2048,128]{1,0:T(8,128)S(1)} %bitcast.9, f32[128,256]{1,0:T(8,128)S(1)} %get-tuple-element.12.w_ref), custom_call_target="tpu_custom_call" | custom-call | tf_op jit(solution)/shard_map/scatter_gradient/pallas_call | solution.py:567
  134.9 1.0 copy.19
  135.9 0.7 broadcast_multiply_fusion
Async XLA Ops:
  0.6 55.7 %copy-start = (bf16[2048,128]{1,0:T(8,128)(2,1)S(1)}, bf16[2048,128]{1,0:T(8,128)(2,1)}, u32[]{:S(2)}) copy-start(bf16[2048,128]{1,0:T(8,128)(2,1)} %x_ref.1) | copy-start | bytes 1572868
  0.6 55.7 %copy-start.1 = (bf16[16,4,128,128]{3,2,1,0:T(8,128)(2,1)S(1)}, bf16[16,4,128,128]{3,2,1,0:T(8,128)(2,1)}, u32[]{:S(2)}) copy-start(bf16[16,4,128,128]{3,2,1,0:T(8,128)(2,1)} %refs_7_.1) | copy-start | bytes 6291460
  0.7 55.7 %copy-start.3 = (bf16[128,256]{1,0:T(8,128)(2,1)S(1)}, bf16[128,256]{1,0:T(8,128)(2,1)}, u32[]{:S(2)}) copy-start(bf16[128,256]{1,0:T(8,128)(2,1)} %refs_4_.1) | copy-start | bytes 196612
  56.4 1.2 copy-start.2

commit v2 on v1

--- a/solution.py
+++ b/solution.py
@@ -231,46 +231,51 @@
     )(x)
 
 
-def layer_kernel(
-    tiles_row,
-    lcol,
-    rcol,
-    flag,
-    x_ref,
-    *refs,
-):
-    far = refs[:tiles_row]
-    weight_ref, grad_ref, lv_ref, rv_ref, hidden_ref, part_ref, base_ref, wg_ref = refs[tiles_row:]
-    r = pl.program_id(0)
+def layer_kernel(rows_step, lcol, owner, index, flag, x_ref, *refs):
+    tiles_row = flag.shape[1]
+    far = refs[: rows_step * tiles_row]
+    refs = refs[rows_step * tiles_row :]
+    weight_ref, grad_ref, lv_ref, rv_ref, hidden_ref, part_ref, base_ref, wg_ref = refs
+    first = pl.program_id(0) * rows_step
+    blocks_dev, block, feat = x_ref.shape
     lb = lv_ref.shape[1]
-    block, feat = lv_ref.shape[2], x_ref.shape[2]
     f32, bf16 = jnp.float32, jnp.bfloat16
 
-    @pl.when(r == 0)
+    @pl.when(first == 0)
     def _():
         base_ref[...] = jnp.zeros_like(base_ref)
         wg_ref[...] = jnp.zeros_like(wg_ref)
 
         def clear(i, c):
-            part_ref[i] = jnp.zeros(part_ref.shape[1:], bf16)
+            at = pl.ds(pl.multiple_of(i * 8, 8), 8)
+            part_ref[at] = jnp.zeros((8,) + part_ref.shape[1:], bf16)
             return c
 
-        lax.fori_loop(0, part_ref.shape[0], clear, 0)
+        lax.fori_loop(0, part_ref.shape[0] // 8, clear, 0)
 
     ones = jnp.ones((block, feat), bf16)
-    flags = [flag[r * tiles_row + t].astype(f32) for t in range(tiles_row)]
-    tiles = [lv_ref[0, l] for l in range(lb)] + [rv_ref[0, t] for t in range(tiles_row)]
-    blocks = [jnp.concatenate([x_ref[lcol[r * lb + l]], ones], axis=1) for l in range(lb)]
-    for t in range(tiles_row):
-        seen = jnp.concatenate([far[t][0], ones], axis=1)
-        blocks.append((seen.astype(f32) * flags[t]).astype(bf16))
-    total = jnp.dot(
-        jnp.concatenate(tiles, axis=1),
-        jnp.concatenate(blocks, axis=0),
-        preferred_element_type=f32,
-    )
-    agg = (x_ref[r].astype(f32) + total[:, :feat]).astype(bf16)
-    norm = lax.rsqrt(1.0 + total[:, feat:])
+    flags = [
+        [flag[first + i, t].astype(f32) for t in range(tiles_row)] for i in range(rows_step)
+    ]
+    rows = [
+        jnp.concatenate(
+            [lv_ref[i, l] for l in range(lb)] + [rv_ref[i, t] for t in range(tiles_row)], axis=1
+        )
+        for i in range(rows_step)
+    ]
+    aggs, norms = [], []
+    for i in range(rows_step):
+        blocks = [
+            jnp.concatenate([x_ref[lcol[first + i, l]], ones], axis=1) for l in range(lb)
+        ]
+        for t in range(tiles_row):
+            seen = jnp.concatenate([far[i * tiles_row + t][0], ones], axis=1)
+            blocks.append((seen.astype(f32) * flags[i][t]).astype(bf16))
+        total = jnp.dot(rows[i], jnp.concatenate(blocks, axis=0), preferred_element_type=f32)
+        aggs.append((x_ref[first + i].astype(f32) + total[:, :feat]).astype(bf16))
+        norms.append(lax.rsqrt(1.0 + total[:, feat:]))
+    agg = jnp.concatenate(aggs, axis=0)
+    norm = jnp.concatenate(norms, axis=0)
     hid = weight_ref.shape[1]
     norm = jnp.concatenate([norm] * (hid // feat), axis=1)
     v = norm * jnp.dot(agg, weight_ref[...], preferred_element_type=f32)
@@ -281,44 +286,52 @@
     hidden_ref[...] = (v * half).astype(bf16)
     slope = half + (0.5 * scale) * v * (1.0 - t * t) * (1.0 + (3 * 0.044715) * square)
     gs = (norm * (grad_ref[...].astype(f32) * slope)).astype(bf16)
-    wg_ref[...] += lax.dot_general(agg, gs, (((0,), (0,)), ((), ())), preferred_element_type=f32)
     dagg = lax.dot_general(
         weight_ref[...], gs, (((1,), (1,)), ((), ())), preferred_element_type=f32
     ).astype(bf16)
-    base_ref[r] += dagg.astype(f32)
-    terms = jnp.dot(dagg, jnp.concatenate(tiles, axis=1), preferred_element_type=f32)
-    for l in range(lb):
-        base_ref[lcol[r * lb + l]] += terms[:, l * block : (l + 1) * block]
-    for t in range(tiles_row):
-        at = rcol[r * tiles_row + t]
-        term = terms[:, (lb + t) * block : (lb + t + 1) * block] * flags[t]
-        part_ref[at] = (part_ref[at].astype(f32) + term).astype(bf16)
-
-
-def layer(x, seen, weight, grad_out, local_vals, remote_vals, lcol, rcol, flag):
+    wg_ref[...] += lax.dot_general(agg, gs, (((0,), (0,)), ((), ())), preferred_element_type=f32)
+    for i in range(rows_step):
+        down = dagg[:, i * block : (i + 1) * block]
+        base_ref[first + i] += down.astype(f32)
+        terms = jnp.dot(down, rows[i], preferred_element_type=f32)
+        for l in range(lb):
+            base_ref[lcol[first + i, l]] += terms[:, l * block : (l + 1) * block]
+        for t in range(tiles_row):
+            at = owner[first + i, t] * blocks_dev + index[first + i, t]
+            term = terms[:, (lb + t) * block : (lb + t + 1) * block] * flags[i][t]
+            part_ref[at] = (part_ref[at].astype(f32) + term).astype(bf16)
+
+
+def layer(x, seen, weight, grad_out, local_vals, remote_vals, lcol, owner, index, flag):
     blocks_dev, lb, block, _ = local_vals.shape
     tiles_row = remote_vals.shape[1]
     feat, hid = weight.shape
+    rows_step = 4
     whole = lambda *shape: pl.BlockSpec(shape, lambda r, *_: (0,) * len(shape))
-    far = [
-        pl.BlockSpec((1, block, feat), lambda r, lc, rc, fl, t=t: (rc[r * tiles_row + t], 0, 0))
-        for t in range(tiles_row)
-    ]
+
+    def seen_block(i, t):
+        def at(r, lc, ow, ix, fl):
+            row = r * rows_step + i
+            return ow[row, t] * blocks_dev + ix[row, t], 0, 0
+
+        return pl.BlockSpec((1, block, feat), at)
+
+    far = [seen_block(i, t) for i in range(rows_step) for t in range(tiles_row)]
     return pl.pallas_call(
-        functools.partial(layer_kernel, tiles_row),
+        functools.partial(layer_kernel, rows_step),
         grid_spec=pltpu.PrefetchScalarGridSpec(
-            num_scalar_prefetch=3,
-            grid=(blocks_dev,),
+            num_scalar_prefetch=4,
+            grid=(blocks_dev // rows_step,),
             in_specs=[whole(blocks_dev, block, feat)]
             + far
             + [
                 whole(feat, hid),
-                pl.BlockSpec((block, hid), lambda r, *_: (r, 0)),
-                pl.BlockSpec((1, lb, block, block), lambda r, *_: (r, 0, 0, 0)),
-                pl.BlockSpec((1, tiles_row, block, block), lambda r, *_: (r, 0, 0, 0)),
+                pl.BlockSpec((rows_step * block, hid), lambda r, *_: (r, 0)),
+                pl.BlockSpec((rows_step, lb, block, block), lambda r, *_: (r, 0, 0, 0)),
+                pl.BlockSpec((rows_step, tiles_row, block, block), lambda r, *_: (r, 0, 0, 0)),
             ],
             out_specs=[
-                pl.BlockSpec((block, hid), lambda r, *_: (r, 0)),
+                pl.BlockSpec((rows_step * block, hid), lambda r, *_: (r, 0)),
                 whole(seen.shape[0], feat, block),
                 whole(blocks_dev, feat, block),
                 whole(feat, hid),
@@ -334,7 +347,18 @@
             dimension_semantics=("arbitrary",), vmem_limit_bytes=48 << 20
         ),
         name="layer",
-    )(lcol, rcol, flag, x, *([seen] * tiles_row), weight, grad_out, local_vals, remote_vals)
+    )(
+        lcol,
+        owner,
+        index,
+        flag,
+        x,
+        *([seen] * (rows_step * tiles_row)),
+        weight,
+        grad_out,
+        local_vals,
+        remote_vals,
+    )
 
 
 def scatter_kernel(
@@ -611,7 +635,6 @@
     nodes, feat = features.shape
     row_count = lax.axis_size("row")
     seen = gather(features, row_count).reshape(row_count * blocks_dev, block, feat)
-    rcol = (remote_owner * blocks_dev + remote_index).reshape(-1)
     hidden, part, base, wterm = layer(
         features.reshape(blocks_dev, block, feat),
         seen,
@@ -619,9 +642,10 @@
         grad_out,
         local_vals,
         remote_vals,
-        local_cols.reshape(-1),
-        rcol,
-        remote_flag.reshape(-1),
+        local_cols,
+        remote_owner,
+        remote_index,
+        remote_flag,
     )
     back, wsum = scatter(
         part.reshape(row_count, nodes, feat), base.reshape(nodes, feat), wterm, row_count

time: 137 us -> 128 us (0.934)
  Pallas kernels: 130 us -> 121 us
    pallas_call x1, Pallas kernels: 23.7 us -> 14.8 us  [layer(): pl.pallas_call(functools.partial(layer_kernel, rows_step), grid_spec=pltp...]
    unnamed x10 -> x12, local copies, waits for them, and re-layouts: 2.76 us -> 4.42 us
where the time goes in v2:
time: 128 us
  Pallas kernels  121 us (95%)
  local copies, waits for them, and re-layouts  5.42 us (4%)
    pallas_call x1, Pallas kernels, scatter(): pl.pallas_call(functools.partial(scatter_kernel, zs), out_shape=[jax.Shap...  53.7 us
    pallas_call x1, Pallas kernels, gather(): pl.pallas_call(functools.partial(gather_kernel, zs), out_shape=jax.ShapeD...  52.9 us
    pallas_call x1, Pallas kernels, layer(): pl.pallas_call(functools.partial(layer_kernel, rows_step), grid_spec=pltp...  14.8 us
    unnamed x12, local copies, waits for them, and re-layouts  4.42 us

profile of v2, /device:TPU:0, one launch (start us, length us, event | category | flops | bytes accessed | tf_op | source)
XLA Modules:
  0.0 128.2 jit_solution(4755191580887079733)
XLA Ops:
  0.6 0.0 copy-start.1
  0.6 0.0 copy-start
  0.7 0.0 copy-start.3
  0.7 0.9 copy.12.lcol
  1.6 0.8 copy.13.owner
  2.3 0.8 copy.14.index
  3.1 0.8 copy.15.flag
  3.8 52.9 %gather_features.1 = bf16[16,2048,128]{2,1,0:T(8,128)(2,1)} custom-call(bf16[2048,128]{1,0:T(8,128)(2,1)} %x_ref.1), custom_call_target="tpu_custom_call" | custom-call | tf_op jit(solution)/shard_map/gather_features/pallas_call | solution.py:219
  56.7 0.0 copy-done.1
  56.7 0.0 copy-done
  56.7 0.0 copy-done.3
  56.7 0.0 copy-start.2
  56.8 1.2 copy-done.2
  58.0 14.8 %layer.1 = (bf16[2048,256]{1,0:T(8,128)(2,1)}, bf16[256,128,128]{2,1,0:T(8,128)(2,1)}, f32[16,128,128]{2,1,0:T(8,128)S(1)}, f32[128,256]{1,0:T(8,128)S(1)}) custom-call(s32[16,8]{1,0:T(8,128)S(1)} %copy.12.lcol, s32[16,4]{1,0:T(8,128)S(1)} %copy.13.owner, s32[16,4]{1,0:T(8,128)S(1)} %copy.14.index, s32[16,4]{1,0:T(8,128)S(1)} %copy.15.flag, ...), custom_call_target="tpu_custom_call" | custom-call | tf_op jit(solution)/shard_map/layer/pallas_call | solution.py:320
  72.8 53.7 %scatter_gradient.1 = (bf16[2048,128]{1,0:T(8,128)(2,1)S(1)}, f32[128,256]{1,0:T(8,128)S(1)}) custom-call(bf16[16,2048,128]{2,1,0:T(8,128)(2,1)} %bitcast.27, f32[2048,128]{1,0:T(8,128)S(1)} %bitcast.9, f32[128,256]{1,0:T(8,128)S(1)} %get-tuple-element.12.w_ref), custom_call_target="tpu_custom_call" | custom-call | tf_op jit(solution)/shard_map/scatter_gradient/pallas_call | solution.py:591
  126.5 1.0 copy.16
  127.5 0.7 broadcast_multiply_fusion
Async XLA Ops:
  0.6 56.1 %copy-start.1 = (bf16[2048,128]{1,0:T(8,128)(2,1)S(1)}, bf16[2048,128]{1,0:T(8,128)(2,1)}, u32[]{:S(2)}) copy-start(bf16[2048,128]{1,0:T(8,128)(2,1)} %x_ref.1) | copy-start | bytes 1572868
  0.6 56.1 %copy-start = (bf16[16,4,128,128]{3,2,1,0:T(8,128)(2,1)S(1)}, bf16[16,4,128,128]{3,2,1,0:T(8,128)(2,1)}, u32[]{:S(2)}) copy-start(bf16[16,4,128,128]{3,2,1,0:T(8,128)(2,1)} %refs_19_.1) | copy-start | bytes 6291460
  0.7 56.1 %copy-start.3 = (bf16[128,256]{1,0:T(8,128)(2,1)S(1)}, bf16[128,256]{1,0:T(8,128)(2,1)}, u32[]{:S(2)}) copy-start(bf16[128,256]{1,0:T(8,128)(2,1)} %refs_16_.1) | copy-start | bytes 196612
  56.7 1.2 copy-start.2

commit v3 on v2

--- a/solution.py
+++ b/solution.py
@@ -129,9 +129,14 @@
     pl.semaphore_signal(barrier, inc=1, device_id={"row": device}, device_id_type=MESH)
 
 
+def split_rows(nodes):
+    last = nodes * 3 // 16
+    return (nodes - last) // PIECES, last
+
+
 def gather_kernel(zs, x_ref, out_ref, own_sem, send_sem, recv_sem):
     me, core, yy, zz, sib, ynb = place()
-    rows = x_ref.shape[0] // PIECES
+    rows, tail = split_rows(x_ref.shape[0])
     has_left, has_right = zz > 0, zz < zs - 1
 
     barrier = pltpu.get_barrier_semaphore()
@@ -145,14 +150,16 @@
     own.start()
 
     def copy(kind, shard, j, device, mine=False):
-        zt = lax.div(shard, 4)
-        slot = zt if kind != SIBLING else zt + zs * lax.rem(lax.div(shard, 2), 2)
-        cut = pl.ds(pl.multiple_of(j * rows, rows), rows)
+        slot = lax.div(shard, 4) + zs * lax.rem(lax.div(shard, 2), 2)
+        if j is None:
+            cut, j = pl.ds(PIECES * rows, tail), PIECES
+        else:
+            cut = pl.ds(pl.multiple_of(j * rows, 16), rows)
         there = out_ref.at[shard, cut]
         return pltpu.make_async_remote_copy(
             src_ref=x_ref.at[cut] if mine else there,
             dst_ref=there,
-            send_sem=send_sem.at[kind * zs + slot, j],
+            send_sem=send_sem.at[kind, slot, j],
             recv_sem=recv_sem.at[shard, j],
             device_id={"row": device},
             device_id_type=MESH,
@@ -161,7 +168,12 @@
     def each(body):
         lax.fori_loop(0, PIECES, lambda j, c: (body(j), c)[1], 0)
 
+    def valid(sign, k):
+        return zz >= k if sign < 0 else zz + k < zs
+
     def own_sends(act):
+        act(copy(ACROSS, me, None, ynb, True))
+
         def body(j):
             pl.when(has_right)(lambda: act(copy(RIGHT, me, j, me + 4, True)))
             pl.when(has_left)(lambda: act(copy(LEFT, me, j, me - 4, True)))
@@ -169,8 +181,21 @@
             act(copy(SIBLING, me, j, sib, True))
 
         each(body)
+        act(copy(SIBLING, me, None, sib, True))
+
+    def tails_out(act, k):
+        def go(kind, device):
+            act(copy(kind, me, None, device, True))
+            act(copy(kind, ynb, None, device))
+
+        pl.when(jnp.logical_and(has_right, zz == k))(lambda: go(RIGHT, me + 4))
+        pl.when(jnp.logical_and(has_left, zz == zs - 1 - k))(lambda: go(LEFT, me - 4))
 
     def along(act, wait):
+        if wait:
+            copy(SIBLING, ynb, None, sib).wait_recv()
+        act(copy(SIBLING, ynb, None, sib))
+        tails_out(act, 0)
         for k in range(1, zs):
             for sign in (-1, 1):
                 shard = me + sign * 4 * k
@@ -184,7 +209,23 @@
                     act(copy(ACROSS, shard, j, ynb))
                     act(copy(SIBLING, shard, j, sib))
 
-                pl.when(zz >= k if sign < 0 else zz + k < zs)(functools.partial(each, body))
+                pl.when(valid(sign, k))(functools.partial(each, body))
+            tails_out(act, k)
+        for k in range(1, zs):
+            for sign in (-1, 1):
+                onward = has_right if sign < 0 else has_left
+                kind = RIGHT if sign < 0 else LEFT
+
+                @pl.when(valid(sign, k))
+                def _(sign=sign, k=k, onward=onward, kind=kind):
+                    for base in (me, ynb):
+                        shard = base + sign * 4 * k
+                        if wait:
+                            copy(SIBLING, shard, None, sib).wait_recv()
+                        pl.when(onward)(
+                            lambda shard=shard: act(copy(kind, shard, None, me - sign * 4))
+                        )
+                        act(copy(SIBLING, shard, None, sib))
 
     def across(act, wait):
         for k in range(zs):
@@ -198,7 +239,7 @@
                         copy(SIBLING, shard, j, sib).wait_recv()
                     act(copy(SIBLING, shard, j, sib))
 
-                pl.when(zz >= k if sign < 0 else zz + k < zs)(functools.partial(each, body))
+                pl.when(valid(sign, k))(functools.partial(each, body))
 
     start = lambda c: c.start()
     finish = lambda c: c.wait_send()
@@ -208,6 +249,7 @@
     for q in range(2 * zs):
         shard = 2 * q + 1 - core
         each(lambda j, shard=shard: copy(SIBLING, shard, j, sib).wait_recv())
+        copy(SIBLING, shard, None, sib).wait_recv()
     own.wait()
     own_sends(finish)
     along(finish, False)
@@ -223,8 +265,8 @@
         out_specs=pl.BlockSpec(memory_space=pl.ANY),
         scratch_shapes=[
             pltpu.SemaphoreType.DMA,
-            pltpu.SemaphoreType.DMA((5 * zs, PIECES)),
-            pltpu.SemaphoreType.DMA((row_count, PIECES)),
+            pltpu.SemaphoreType.DMA((4, 2 * zs, PIECES + 1)),
+            pltpu.SemaphoreType.DMA((row_count, PIECES + 1)),
         ],
         compiler_params=pltpu.CompilerParams(collective_id=0, has_side_effects=True),
         name="gather_features",
@@ -232,7 +274,7 @@
 
 
 def layer_kernel(rows_step, lcol, owner, index, flag, x_ref, *refs):
-    tiles_row = flag.shape[1]
+    tiles_row = flag.shape[0]
     far = refs[: rows_step * tiles_row]
     refs = refs[rows_step * tiles_row :]
     weight_ref, grad_ref, lv_ref, rv_ref, hidden_ref, part_ref, base_ref, wg_ref = refs
@@ -255,7 +297,7 @@
 
     ones = jnp.ones((block, feat), bf16)
     flags = [
-        [flag[first + i, t].astype(f32) for t in range(tiles_row)] for i in range(rows_step)
+        [flag[t, first + i].astype(f32) for t in range(tiles_row)] for i in range(rows_step)
     ]
     rows = [
         jnp.concatenate(
@@ -266,7 +308,7 @@
     aggs, norms = [], []
     for i in range(rows_step):
         blocks = [
-            jnp.concatenate([x_ref[lcol[first + i, l]], ones], axis=1) for l in range(lb)
+            jnp.concatenate([x_ref[lcol[l, first + i]], ones], axis=1) for l in range(lb)
         ]
         for t in range(tiles_row):
             seen = jnp.concatenate([far[i * tiles_row + t][0], ones], axis=1)
@@ -295,9 +337,9 @@
         base_ref[first + i] += down.astype(f32)
         terms = jnp.dot(down, rows[i], preferred_element_type=f32)
         for l in range(lb):
-            base_ref[lcol[first + i, l]] += terms[:, l * block : (l + 1) * block]
+            base_ref[lcol[l, first + i]] += terms[:, l * block : (l + 1) * block]
         for t in range(tiles_row):
-            at = owner[first + i, t] * blocks_dev + index[first + i, t]
+            at = owner[t, first + i] * blocks_dev + index[t, first + i]
             term = terms[:, (lb + t) * block : (lb + t + 1) * block] * flags[i][t]
             part_ref[at] = (part_ref[at].astype(f32) + term).astype(bf16)
 
@@ -312,7 +354,7 @@
     def seen_block(i, t):
         def at(r, lc, ow, ix, fl):
             row = r * rows_step + i
-            return ow[row, t] * blocks_dev + ix[row, t], 0, 0
+            return ow[t, row] * blocks_dev + ix[t, row], 0, 0
 
         return pl.BlockSpec((1, block, feat), at)
 
@@ -372,6 +414,7 @@
     from_core,
     from_y,
     from_z,
+    tail_z,
     held,
     base_sum,
     w_in,
@@ -381,11 +424,13 @@
     core_sem,
     y_sem,
     z_sem,
+    tail_send,
+    tail_sem,
     w_send,
     w_recv,
 ):
     me, core, yy, zz, sib, ynb = place()
-    rows = part_ref.shape[1] // PIECES
+    rows, tail = split_rows(part_ref.shape[1])
     has_left, has_right = zz > 0, zz < zs - 1
     f32, bf16 = jnp.float32, jnp.bfloat16
     near = me + 4 * (1 - 2 * lax.rem(zz, 2))
@@ -413,7 +458,9 @@
         lax.fori_loop(0, PIECES, lambda j, c: (body(j), c)[1], 0)
 
     def cut(j):
-        return pl.ds(pl.multiple_of(j * rows, rows), rows)
+        if isinstance(j, int):
+            return pl.ds(PIECES * rows, tail)
+        return pl.ds(pl.multiple_of(j * rows, 16), rows)
 
     def remote(src, dst, send, recv, device):
         return pltpu.make_async_remote_copy(
@@ -485,30 +532,97 @@
             device,
         )
 
-    for yt in (1 - yy, yy):
-        for d, sign in order(0):
-            zt = zz + sign * d
-            pl.when(valid(sign, d))(
-                functools.partial(each, lambda j, zt=zt, yt=yt: to_core(zt, yt, j).start())
-            )
-
-    w_go(0)
-    step = 1
-    for d, sign in order(0):
+    def to_next(zt, yt, way, device):
+        q = yt * zs + zt
+        return remote(
+            held.at[q, cut(PIECES)],
+            tail_z.at[way, q],
+            tail_send.at[q],
+            tail_sem.at[way, q],
+            device,
+        )
+
+    def tail_sum(zt, yt):
+        q = yt * zs + zt
+        to_core(zt, yt, PIECES).wait_recv()
+        return mine[q, cut(PIECES)].astype(f32) + from_core[q, cut(PIECES)].astype(f32)
+
+    def core_sends(yt, d, sign):
+        zt = zz + sign * d
+        pl.when(valid(sign, d))(functools.partial(each, lambda j: to_core(zt, yt, j).start()))
+
+    near_first = list(order(0))
+    for d, sign in near_first[:2]:
+        core_sends(1 - yy, d, sign)
+    for d, sign in near_first:
         zt = zz + sign * d
 
         @pl.when(valid(sign, d))
         def _(zt=zt):
-            q = (1 - yy) * zs + zt
-            load(zt, 1 - yy).wait()
-
-            def body(j):
-                to_core(zt, 1 - yy, j).wait_recv()
-                total = mine[q, cut(j)].astype(f32) + from_core[q, cut(j)].astype(f32)
-                held[q, cut(j)] = total.astype(bf16)
-                to_y(zt, j).start()
-
-            each(body)
+            to_core(zt, 1 - yy, PIECES).start()
+            to_core(zt, yy, PIECES).start()
+
+    for d, sign in near_first[2:]:
+        core_sends(1 - yy, d, sign)
+    for d, sign in near_first:
+        core_sends(yy, d, sign)
+
+    w_go(0)
+    for yt in range(2):
+        for zt in range(zs):
+            load(zt, yt).wait()
+
+    for d in range(zs - 1, -1, -1):
+        for sign in (1, -1) if d else (1,):
+            zt = zz + sign * d
+
+            @pl.when(valid(sign, d))
+            def _(zt=zt):
+                q = (1 - yy) * zs + zt
+
+                def body(j):
+                    to_core(zt, 1 - yy, j).wait_recv()
+                    total = mine[q, cut(j)].astype(f32) + from_core[q, cut(j)].astype(f32)
+                    held[q, cut(j)] = total.astype(bf16)
+                    to_y(zt, j).start()
+
+                each(body)
+
+        for sign in (1, -1) if d else ():
+            zt = zz + sign * d
+            way = 0 if sign > 0 else 1
+            behind = has_left if sign > 0 else has_right
+
+            @pl.when(valid(sign, d))
+            def _(zt=zt, way=way, behind=behind, sign=sign):
+                for yt in (1 - yy, yy):
+                    q = yt * zs + zt
+                    total = tail_sum(zt, yt)
+
+                    @pl.when(behind)
+                    def _():
+                        to_next(zt, yt, way, sib).wait_recv()
+                        held[q, cut(PIECES)] = (total + tail_z[way, q].astype(f32)).astype(bf16)
+
+                    @pl.when(jnp.logical_not(behind))
+                    def _():
+                        held[q, cut(PIECES)] = total.astype(bf16)
+
+                    to_next(zt, yt, way, me + sign * 4).start()
+
+    for yt in (1 - yy, yy):
+        q = yt * zs + zz
+        base_sum[cut(PIECES)] = tail_sum(zz, yt)
+        for way, behind in ((0, has_left), (1, has_right)):
+
+            @pl.when(behind)
+            def _(way=way, q=q, yt=yt):
+                to_next(zz, yt, way, sib).wait_recv()
+                base_sum[cut(PIECES)] += tail_z[way, q].astype(f32)
+
+        if yt is not yy:
+            held[q, cut(PIECES)] = base_sum[cut(PIECES)].astype(bf16)
+            to_y(zz, PIECES).start()
 
     def summed(zt, j):
         q = yy * zs + zt
@@ -526,7 +640,6 @@
 
         @pl.when(valid(sign, d))
         def _(zt=zt, way=way, behind=behind, sign=sign):
-            load(zt, yy).wait()
 
             def body(j):
                 total = summed(zt, j)
@@ -549,8 +662,6 @@
             w_go(step)
             step += 1
 
-    load(zz, yy).wait()
-
     def last(j):
         base_sum[cut(j)] = base_ref[cut(j)] + summed(zz, j)
 
@@ -567,12 +678,19 @@
         out_ref[cut(j)] = base_sum[cut(j)].astype(bf16)
 
     each(last)
+    to_y(zz, PIECES).wait_recv()
+    total = base_ref[cut(PIECES)] + base_sum[cut(PIECES)]
+    out_ref[cut(PIECES)] = (total + from_y[zz, cut(PIECES)].astype(f32)).astype(bf16)
 
     w_back.wait_recv()
     for c in w_steps:
         c.wait_send()
     w_last.wait_send()
+    to_y(zz, PIECES).wait_send()
     for zt in range(zs):
+        for yt in range(2):
+            to_core(zt, yt, PIECES).wait_send()
+            pl.when(zz != zt)(lambda zt=zt, yt=yt: to_next(zt, yt, 0, sib).wait_send())
         each(lambda j, zt=zt: to_core(zt, 0, j).wait_send())
         each(lambda j, zt=zt: to_core(zt, 1, j).wait_send())
         each(lambda j, zt=zt: to_y(zt, j).wait_send())
@@ -601,15 +719,18 @@
             shard(2 * zs),
             shard(zs),
             shard(2, zs),
+            pltpu.VMEM((2, 2 * zs, split_rows(nodes)[1], feat), jnp.bfloat16),
             shard(2 * zs),
             pltpu.VMEM((nodes, feat), jnp.float32),
             pltpu.VMEM((4,) + wshape, jnp.float32),
             pltpu.VMEM((3,) + wshape, jnp.float32),
             dma((2 * zs,)),
-            dma((4 * zs, PIECES)),
-            dma((2 * zs, PIECES)),
-            dma((zs, PIECES)),
+            dma((4 * zs, PIECES + 1)),
+            dma((2 * zs, PIECES + 1)),
+            dma((zs, PIECES + 1)),
             dma((2, zs, PIECES)),
+            dma((2 * zs,)),
+            dma((2, 2 * zs)),
             dma((5,)),
             dma((5,)),
         ],
@@ -642,10 +763,10 @@
         grad_out,
         local_vals,
         remote_vals,
-        local_cols,
-        remote_owner,
-        remote_index,
-        remote_flag,
+        local_cols.T,
+        remote_owner.T,
+        remote_index.T,
+        remote_flag.T,
     )
     back, wsum = scatter(
         part.reshape(row_count, nodes, feat), base.reshape(nodes, feat), wterm, row_count

time: 128 us -> 124 us (0.969)
  local copies, waits for them, and re-layouts: 5.42 us -> 2.26 us
    unnamed x12 -> x16, local copies, waits for them, and re-layouts: 4.42 us -> 1.25 us
where the time goes in v3:
time: 124 us; the launch traced here: 123 us
  Pallas kernels  120 us (97%)
  local copies, waits for them, and re-layouts  2.26 us (2%)
    pallas_call x1, Pallas kernels, scatter(): pl.pallas_call(functools.partial(scatter_kernel, zs), out_shape=[jax.Shap...  53.3 us
    pallas_call x1, Pallas kernels, gather(): pl.pallas_call(functools.partial(gather_kernel, zs), out_shape=jax.ShapeD...  51.8 us
    pallas_call x1, Pallas kernels, layer(): pl.pallas_call(functools.partial(layer_kernel, rows_step), grid_spec=pltp...  14.6 us

profile of v3, /device:TPU:0, one launch (start us, length us, event | category | flops | bytes accessed | tf_op | source)
XLA Modules:
  0.0 123.4 jit_solution(11991065095529062783)
XLA Ops:
  0.6 0.0 copy-start.1
  0.6 0.0 copy-start.7
  0.7 0.0 copy-start.6
  0.7 0.0 copy-start.5
  0.7 0.0 copy-start
  0.7 0.0 copy-start.4
  0.7 0.0 copy-start.3
  0.7 51.8 %gather_features.1 = bf16[16,2048,128]{2,1,0:T(8,128)(2,1)} custom-call(bf16[2048,128]{1,0:T(8,128)(2,1)} %x_ref.1), custom_call_target="tpu_custom_call" | custom-call | tf_op jit(solution)/shard_map/gather_features/pallas_call | solution.py:261
  52.6 0.0 copy-done.1
  52.6 0.0 copy-done.7
  52.6 0.0 copy-done.6
  52.6 0.0 copy-done.5
  52.6 0.0 copy-done
  52.6 0.0 copy-done.4
  52.6 0.0 copy-done.3
  52.6 0.0 copy-start.2
  52.6 1.2 copy-done.2
  53.9 14.6 %layer.1 = (bf16[2048,256]{1,0:T(8,128)(2,1)}, bf16[256,128,128]{2,1,0:T(8,128)(2,1)}, f32[16,128,128]{2,1,0:T(8,128)S(1)}, f32[128,256]{1,0:T(8,128)S(1)}) custom-call(s32[8,16]{1,0:T(8,128)S(1)} %bitcast.15, s32[4,16]{1,0:T(4,128)S(1)} %bitcast.16, s32[4,16]{1,0:T(4,128)S(1)} %bitcast.17, s32[4,16]{1,0:T(4,128)S(1)} %bitcast.18, ...), custom_call_target="tpu_custom_call" | custom-call | tf_op jit(solution)/shard_map/layer/pallas_call | solution.py:362
  68.4 53.3 %scatter_gradient.1 = (bf16[2048,128]{1,0:T(8,128)(2,1)S(1)}, f32[128,256]{1,0:T(8,128)S(1)}) custom-call(bf16[16,2048,128]{2,1,0:T(8,128)(2,1)} %bitcast.35, f32[2048,128]{1,0:T(8,128)S(1)} %bitcast.13, f32[128,256]{1,0:T(8,128)S(1)} %get-tuple-element.12.w_ref), custom_call_target="tpu_custom_call" | custom-call | tf_op jit(solution)/shard_map/scatter_gradient/pallas_call | solution.py:709
  121.7 1.0 copy.12
  122.7 0.7 broadcast_multiply_fusion
Async XLA Ops:
  0.6 51.9 %copy-start.1 = (bf16[2048,128]{1,0:T(8,128)(2,1)S(1)}, bf16[2048,128]{1,0:T(8,128)(2,1)}, u32[]{:S(2)}) copy-start(bf16[2048,128]{1,0:T(8,128)(2,1)} %x_ref.1) | copy-start | bytes 1572868
  0.6 51.9 %copy-start.7 = (s32[16,4]{0,1:T(4,128)S(1)}, s32[16,4]{0,1:T(4,128)}, u32[]{:S(2)}) copy-start(s32[16,4]{0,1:T(4,128)} %param.17) | copy-start | bytes 772
  0.7 51.9 %copy-start.6 = (s32[16,4]{0,1:T(4,128)S(1)}, s32[16,4]{0,1:T(4,128)}, u32[]{:S(2)}) copy-start(s32[16,4]{0,1:T(4,128)} %param.16) | copy-start | bytes 772
  0.7 51.9 %copy-start.5 = (s32[16,4]{0,1:T(4,128)S(1)}, s32[16,4]{0,1:T(4,128)}, u32[]{:S(2)}) copy-start(s32[16,4]{0,1:T(4,128)} %param.15) | copy-start | bytes 772
  0.7 51.9 %copy-start = (bf16[16,4,128,128]{3,2,1,0:T(8,128)(2,1)S(1)}, bf16[16,4,128,128]{3,2,1,0:T(8,128)(2,1)}, u32[]{:S(2)}) copy-start(bf16[16,4,128,128]{3,2,1,0:T(8,128)(2,1)} %refs_19_.1) | copy-start | bytes 6291460
  0.7 51.9 %copy-start.4 = (s32[16,8]{0,1:T(8,128)S(1)}, s32[16,8]{0,1:T(8,128)}, u32[]{:S(2)}) copy-start(s32[16,8]{0,1:T(8,128)} %param.13) | copy-start | bytes 1540
  0.7 51.9 %copy-start.3 = (bf16[128,256]{1,0:T(8,128)(2,1)S(1)}, bf16[128,256]{1,0:T(8,128)(2,1)}, u32[]{:S(2)}) copy-start(bf16[128,256]{1,0:T(8,128)(2,1)} %refs_16_.1) | copy-start | bytes 196612
  52.6 1.2 copy-start.2

commit v4 on v3

--- a/solution.py
+++ b/solution.py
@@ -130,7 +130,7 @@
 
 
 def split_rows(nodes):
-    last = nodes * 3 // 16
+    last = nodes // 8
     return (nodes - last) // PIECES, last
 
 
@@ -386,7 +386,7 @@
             jax.ShapeDtypeStruct((feat, hid), jnp.float32),
         ],
         compiler_params=pltpu.CompilerParams(
-            dimension_semantics=("arbitrary",), vmem_limit_bytes=48 << 20
+            dimension_semantics=("arbitrary",), vmem_limit_bytes=28 << 20
         ),
         name="layer",
     )(
@@ -735,7 +735,7 @@
             dma((5,)),
         ],
         compiler_params=pltpu.CompilerParams(
-            collective_id=1, has_side_effects=True, vmem_limit_bytes=48 << 20
+            collective_id=1, has_side_effects=True, vmem_limit_bytes=24 << 20
         ),
         name="scatter_gradient",
     )(part, base, wterm)

time: 124 us -> 122 us (0.984)
  Pallas kernels: 120 us -> 112 us
  local copies, waits for them, and re-layouts: 2.26 us -> 7.82 us
    unnamed x16 -> x20, local copies, waits for them, and re-layouts: 1.25 us -> 6.82 us
    pallas_call x1, Pallas kernels: 14.6 us -> 9.57 us  [layer(): pl.pallas_call(functools.partial(layer_kernel, rows_step), grid_spec=pltp...]
    pallas_call x1, Pallas kernels: 51.8 us -> 49.9 us  [gather(): pl.pallas_call(functools.partial(gather_kernel, zs), out_shape=jax.ShapeD...]
where the time goes in v4:
time: 122 us
  Pallas kernels  112 us (92%)
  local copies, waits for them, and re-layouts  7.82 us (6%)
    pallas_call x1, Pallas kernels, scatter(): pl.pallas_call(functools.partial(scatter_kernel, zs), out_shape=[jax.Shap...  52.8 us
    pallas_call x1, Pallas kernels, gather(): pl.pallas_call(functools.partial(gather_kernel, zs), out_shape=jax.ShapeD...  49.9 us
    pallas_call x1, Pallas kernels, layer(): pl.pallas_call(functools.partial(layer_kernel, rows_step), grid_spec=pltp...  9.57 us
    unnamed x20, local copies, waits for them, and re-layouts  6.82 us

profile of v4, /device:TPU:0, one launch (start us, length us, event | category | flops | bytes accessed | tf_op | source)
XLA Modules:
  0.0 121.5 jit_solution(8198751283293358060)
XLA Ops:
  0.6 0.0 copy-start.3
  0.6 0.0 copy-start.9
  0.7 0.0 copy-start.8
  0.7 0.0 copy-start.7
  0.7 0.0 copy-start.2
  0.7 0.0 copy-start.6
  0.7 0.0 copy-start.5
  0.7 49.9 %gather_features.1 = bf16[16,2048,128]{2,1,0:T(8,128)(2,1)} custom-call(bf16[2048,128]{1,0:T(8,128)(2,1)} %x_ref.1), custom_call_target="tpu_custom_call" | custom-call | tf_op jit(solution)/shard_map/gather_features/pallas_call | solution.py:261
  50.6 0.0 copy-done.3
  50.6 0.0 copy-done.9
  50.6 0.0 copy-done.8
  50.6 0.0 copy-done.7
  50.6 0.0 copy-done.2
  50.6 0.0 copy-done.6
  50.6 0.0 copy-done.5
  50.7 0.0 copy-start
  50.7 3.4 %copy-done = bf16[16,2048,128]{2,1,0:T(8,128)(2,1)S(1)} copy-done((bf16[16,2048,128]{2,1,0:T(8,128)(2,1)S(1)}, bf16[16,2048,128]{2,1,0:T(8,128)(2,1)}, u32[]{:S(2)}) %copy-start) | copy-done | bytes 8388632
  54.0 0.0 copy-start.1
  54.0 2.2 %copy-done.1 = bf16[16,8,128,128]{3,2,1,0:T(8,128)(2,1)S(1)} copy-done((bf16[16,8,128,128]{3,2,1,0:T(8,128)(2,1)S(1)}, bf16[16,8,128,128]{3,2,1,0:T(8,128)(2,1)}, u32[]{:S(2)}) %copy-start.1) | copy-done | bytes 4194328
  56.2 0.0 copy-start.4
  56.2 1.2 %copy-done.4 = bf16[2048,256]{1,0:T(8,128)(2,1)S(1)} copy-done((bf16[2048,256]{1,0:T(8,128)(2,1)S(1)}, bf16[2048,256]{1,0:T(8,128)(2,1)}, u32[]{:S(2)}) %copy-start.4) | copy-done | bytes 1048600
  57.5 9.6 %layer.1 = (bf16[2048,256]{1,0:T(8,128)(2,1)}, bf16[256,128,128]{2,1,0:T(8,128)(2,1)S(1)}, f32[16,128,128]{2,1,0:T(8,128)S(1)}, f32[128,256]{1,0:T(8,128)S(1)}) custom-call(s32[8,16]{1,0:T(8,128)S(1)} %bitcast.32, s32[4,16]{1,0:T(4,128)S(1)} %bitcast.33, s32[4,16]{1,0:T(4,128)S(1)} %bitcast.34, s32[4,16]{1,0:T(4,128)S(1)} %bitcast.35, ...), custom_call_target="tpu_custom_call" | custom-call | tf_op jit(solution)/shard_map/layer/pallas_call | solution.py:362
  67.0 52.8 %scatter_gradient.1 = (bf16[2048,128]{1,0:T(8,128)(2,1)S(1)}, f32[128,256]{1,0:T(8,128)S(1)}) custom-call(bf16[16,2048,128]{2,1,0:T(8,128)(2,1)S(1)} %bitcast.28, f32[2048,128]{1,0:T(8,128)S(1)} %bitcast.30, f32[128,256]{1,0:T(8,128)S(1)} %get-tuple-element.12.w_ref), custom_call_target="tpu_custom_call" | custom-call | tf_op jit(solution)/shard_map/scatter_gradient/pallas_call | solution.py:709
  119.8 1.0 copy.12
  120.8 0.7 broadcast_multiply_fusion
Async XLA Ops:
  0.6 50.0 %copy-start.3 = (bf16[2048,128]{1,0:T(8,128)(2,1)S(1)}, bf16[2048,128]{1,0:T(8,128)(2,1)}, u32[]{:S(2)}) copy-start(bf16[2048,128]{1,0:T(8,128)(2,1)} %x_ref.1) | copy-start | bytes 1572868
  0.6 50.0 %copy-start.9 = (s32[16,4]{0,1:T(4,128)S(1)}, s32[16,4]{0,1:T(4,128)}, u32[]{:S(2)}) copy-start(s32[16,4]{0,1:T(4,128)} %param.17) | copy-start | bytes 772
  0.7 50.0 %copy-start.8 = (s32[16,4]{0,1:T(4,128)S(1)}, s32[16,4]{0,1:T(4,128)}, u32[]{:S(2)}) copy-start(s32[16,4]{0,1:T(4,128)} %param.16) | copy-start | bytes 772
  0.7 50.0 %copy-start.7 = (s32[16,4]{0,1:T(4,128)S(1)}, s32[16,4]{0,1:T(4,128)}, u32[]{:S(2)}) copy-start(s32[16,4]{0,1:T(4,128)} %param.15) | copy-start | bytes 772
  0.7 50.0 %copy-start.2 = (bf16[16,4,128,128]{3,2,1,0:T(8,128)(2,1)S(1)}, bf16[16,4,128,128]{3,2,1,0:T(8,128)(2,1)}, u32[]{:S(2)}) copy-start(bf16[16,4,128,128]{3,2,1,0:T(8,128)(2,1)} %refs_19_.1) | copy-start | bytes 6291460
  0.7 50.0 %copy-start.6 = (s32[16,8]{0,1:T(8,128)S(1)}, s32[16,8]{0,1:T(8,128)}, u32[]{:S(2)}) copy-start(s32[16,8]{0,1:T(8,128)} %param.13) | copy-start | bytes 1540
  0.7 50.0 %copy-start.5 = (bf16[128,256]{1,0:T(8,128)(2,1)S(1)}, bf16[128,256]{1,0:T(8,128)(2,1)}, u32[]{:S(2)}) copy-start(bf16[128,256]{1,0:T(8,128)(2,1)} %refs_16_.1) | copy-start | bytes 196612
  50.7 3.4 %copy-start = (bf16[16,2048,128]{2,1,0:T(8,128)(2,1)S(1)}, bf16[16,2048,128]{2,1,0:T(8,128)(2,1)}, u32[]{:S(2)}) copy-start(bf16[16,2048,128]{2,1,0:T(8,128)(2,1)} %gather_features.1) | copy-start | bytes 25165828
  54.0 2.2 %copy-start.1 = (bf16[16,8,128,128]{3,2,1,0:T(8,128)(2,1)S(1)}, bf16[16,8,128,128]{3,2,1,0:T(8,128)(2,1)}, u32[]{:S(2)}) copy-start(bf16[16,8,128,128]{3,2,1,0:T(8,128)(2,1)} %refs_18_.1) | copy-start | bytes 12582916
  56.2 1.2 %copy-start.4 = (bf16[2048,256]{1,0:T(8,128)(2,1)S(1)}, bf16[2048,256]{1,0:T(8,128)(2,1)}, u32[]{:S(2)}) copy-start(bf16[2048,256]{1,0:T(8,128)(2,1)} %refs_17_.1) | copy-start | bytes 3145732

commit v5 on v4

--- a/solution.py
+++ b/solution.py
@@ -268,7 +268,12 @@
             pltpu.SemaphoreType.DMA((4, 2 * zs, PIECES + 1)),
             pltpu.SemaphoreType.DMA((row_count, PIECES + 1)),
         ],
-        compiler_params=pltpu.CompilerParams(collective_id=0, has_side_effects=True),
+        compiler_params=pltpu.CompilerParams(
+            collective_id=0, has_side_effects=True, vmem_limit_bytes=2 << 20
+        ),
+        cost_estimate=pl.CostEstimate(
+            flops=1 << 35, bytes_accessed=64 * x.shape[0] * x.shape[1], transcendentals=0
+        ),
         name="gather_features",
     )(x)
 

time: 122 us -> 115 us (0.943)
  local copies, waits for them, and re-layouts: 7.82 us -> 2.08 us
    unnamed x20, local copies, waits for them, and re-layouts: 6.82 us -> 1.07 us
where the time goes in v5:
time: 115 us
  Pallas kernels  112 us (97%)
  local copies, waits for them, and re-layouts  2.08 us (2%)
    pallas_call x1, Pallas kernels, scatter(): pl.pallas_call(functools.partial(scatter_kernel, zs), out_shape=[jax.Shap...  53.1 us
    pallas_call x1, Pallas kernels, gather(): pl.pallas_call(functools.partial(gather_kernel, zs), out_shape=jax.ShapeD...  49 us
    pallas_call x1, Pallas kernels, layer(): pl.pallas_call(functools.partial(layer_kernel, rows_step), grid_spec=pltp...  9.58 us

profile of v5, /device:TPU:0, one launch (start us, length us, event | category | flops | bytes accessed | tf_op | source)
XLA Modules:
  0.0 115.2 jit_solution(15217938293446132332)
XLA Ops:
  0.6 0.0 copy-start.3
  0.6 1.0 copy-done.3
  1.7 0.0 copy-start
  1.7 0.0 copy-start.1
  1.7 0.0 copy-start.2
  1.7 0.0 copy-start.4
  1.7 0.0 copy-start.5
  1.7 0.0 copy-start.6
  1.7 0.0 copy-start.7
  1.7 0.0 copy-start.8
  1.7 0.0 copy-start.9
  1.7 49.0 %gather_features.1 = bf16[16,2048,128]{2,1,0:T(8,128)(2,1)S(1)} custom-call(bf16[2048,128]{1,0:T(8,128)(2,1)S(1)} %copy-done.3), custom_call_target="tpu_custom_call" | custom-call | flops 34359738368 | bytes 16777216 | tf_op jit(solution)/shard_map/gather_features/pallas_call | solution.py:261
  50.7 0.0 copy-done
  50.7 0.0 copy-done.1
  50.7 0.0 copy-done.2
  50.7 0.0 copy-done.4
  50.7 0.0 copy-done.5
  50.8 0.0 copy-done.6
  50.8 0.0 copy-done.7
  50.8 0.0 copy-done.8
  50.8 0.0 copy-done.9
  50.8 9.6 %layer.1 = (bf16[2048,256]{1,0:T(8,128)(2,1)}, bf16[256,128,128]{2,1,0:T(8,128)(2,1)S(1)}, f32[16,128,128]{2,1,0:T(8,128)S(1)}, f32[128,256]{1,0:T(8,128)S(1)}) custom-call(s32[8,16]{1,0:T(8,128)S(1)} %bitcast.32, s32[4,16]{1,0:T(4,128)S(1)} %bitcast.33, s32[4,16]{1,0:T(4,128)S(1)} %bitcast.34, s32[4,16]{1,0:T(4,128)S(1)} %bitcast.35, ...), custom_call_target="tpu_custom_call" | custom-call | tf_op jit(solution)/shard_map/layer/pallas_call | solution.py:367
  60.4 53.1 %scatter_gradient.1 = (bf16[2048,128]{1,0:T(8,128)(2,1)S(1)}, f32[128,256]{1,0:T(8,128)S(1)}) custom-call(bf16[16,2048,128]{2,1,0:T(8,128)(2,1)S(1)} %bitcast.28, f32[2048,128]{1,0:T(8,128)S(1)} %bitcast.29, f32[128,256]{1,0:T(8,128)S(1)} %get-tuple-element.12.w_ref), custom_call_target="tpu_custom_call" | custom-call | tf_op jit(solution)/shard_map/scatter_gradient/pallas_call | solution.py:714
  113.5 1.0 copy.12
  114.5 0.7 broadcast_multiply_fusion
Async XLA Ops:
  0.6 1.0 copy-start.3
  1.7 49.0 %copy-start = (bf16[16,8,128,128]{3,2,1,0:T(8,128)(2,1)S(1)}, bf16[16,8,128,128]{3,2,1,0:T(8,128)(2,1)}, u32[]{:S(2)}) copy-start(bf16[16,8,128,128]{3,2,1,0:T(8,128)(2,1)} %refs_18_.1) | copy-start | bytes 12582916
  1.7 49.0 %copy-start.1 = (bf16[16,4,128,128]{3,2,1,0:T(8,128)(2,1)S(1)}, bf16[16,4,128,128]{3,2,1,0:T(8,128)(2,1)}, u32[]{:S(2)}) copy-start(bf16[16,4,128,128]{3,2,1,0:T(8,128)(2,1)} %refs_19_.1) | copy-start | bytes 6291460
  1.7 49.0 %copy-start.2 = (bf16[2048,256]{1,0:T(8,128)(2,1)S(1)}, bf16[2048,256]{1,0:T(8,128)(2,1)}, u32[]{:S(2)}) copy-start(bf16[2048,256]{1,0:T(8,128)(2,1)} %refs_17_.1) | copy-start | bytes 3145732
  1.7 49.1 %copy-start.4 = (bf16[2048,128]{1,0:T(8,128)(2,1)S(1)}, bf16[2048,128]{1,0:T(8,128)(2,1)}, u32[]{:S(2)}) copy-start(bf16[2048,128]{1,0:T(8,128)(2,1)} %x_ref.1) | copy-start | bytes 1572868
  1.7 49.1 %copy-start.5 = (bf16[128,256]{1,0:T(8,128)(2,1)S(1)}, bf16[128,256]{1,0:T(8,128)(2,1)}, u32[]{:S(2)}) copy-start(bf16[128,256]{1,0:T(8,128)(2,1)} %refs_16_.1) | copy-start | bytes 196612
  1.7 49.1 %copy-start.6 = (s32[16,8]{0,1:T(8,128)S(1)}, s32[16,8]{0,1:T(8,128)}, u32[]{:S(2)}) copy-start(s32[16,8]{0,1:T(8,128)} %param.13) | copy-start | bytes 1540
  1.7 49.1 %copy-start.7 = (s32[16,4]{0,1:T(4,128)S(1)}, s32[16,4]{0,1:T(4,128)}, u32[]{:S(2)}) copy-start(s32[16,4]{0,1:T(4,128)} %param.15) | copy-start | bytes 772
  1.7 49.1 %copy-start.8 = (s32[16,4]{0,1:T(4,128)S(1)}, s32[16,4]{0,1:T(4,128)}, u32[]{:S(2)}) copy-start(s32[16,4]{0,1:T(4,128)} %param.16) | copy-start | bytes 772
  1.7 49.1 %copy-start.9 = (s32[16,4]{0,1:T(4,128)S(1)}, s32[16,4]{0,1:T(4,128)}, u32[]{:S(2)}) copy-start(s32[16,4]{0,1:T(4,128)} %param.17) | copy-start | bytes 772
